TPU v7x, 128 devices: a whole 4x4x4 slice. The times are simulated.
128 devices in a mesh: tile: 4 (over x), dev: 32 (over z, y, core).
Axes of the slice: x: 4, y: 4, z: 4, core: 2. Of those that a mesh axis runs over, the one named last changes fastest.
Arguments:
- u_field: float32 [256, 256, 1024], P('dev', 'tile'), may hold values from 0.2 to 1
- v_field: float32 [256, 256, 1024], P('dev', 'tile'), may hold values from 0 to 1
- brick_material: int32 [4, 4, 16], replicated, may hold values from 0 to 3
- color_table: float32 [4, 3, 16], replicated, may hold values from 0 to 2
- alpha_table: float32 [4, 16], replicated, may hold values from 0.002 to 0.02
- assign: int32 [32], replicated, may hold values from 0 to 31, as said below
Outputs:
- u_out: float32 [256, 256, 1024], P('dev', 'tile')
- v_out: float32 [256, 256, 1024], P('dev', 'tile')
- image: float32 [3, 256, 1024], P(None, ('tile', 'dev'))
Inputs may be any that keep to these rules, and one draw needn't show every extreme that they name: `assign`: every row block appears once; output blocks g * 8 to g * 8 + 7 take exactly 2 blocks from each brick owner (blocks o * 8 to o * 8 + 7).
All inputs are finite; a program needn't handle non-finite values.
Results may differ from a plain program's by a relative error of at most 0.00039.
Values may be sent and summed in bfloat16 or wider, within the bound.
A program may use at most 384 MiB of HBM per device.

v0:
```python
import jax
import jax.numpy as jnp
from jax import lax
from jax.sharding import PartitionSpec as P

RB = 8
BK = 64


def extended(cells, sides, width):
    for axis, dim in sides:
        count = lax.axis_size(axis)
        ends = count - 1
        head = lax.slice_in_dim(cells, 0, width, axis=dim)
        tail = lax.slice_in_dim(cells, cells.shape[dim] - width, cells.shape[dim], axis=dim)
        cells = jnp.concatenate(
            [
                lax.ppermute(tail, axis, [(i, (i + 1) % count) for i in range(ends)]),
                cells,
                lax.ppermute(head, axis, [((i + 1) % count, i) for i in range(ends)]),
            ],
            axis=dim,
        )
    return cells


def laplace(field):
    centre = field[1:-1, 1:-1]
    sides = jnp.pad(centre, ((0, 0), (0, 0), (1, 1)))
    total = field[2:, 1:-1] + field[:-2, 1:-1] + field[1:-1, 2:] + field[1:-1, :-2]
    total = total + sides[:, :, 2:] + sides[:, :, :-2]
    return total - 6.0 * centre


def react_diffuse(subst, activ):
    s_mid = subst[1:-1, 1:-1]
    a_mid = activ[1:-1, 1:-1]
    feeding = s_mid * a_mid * a_mid
    s_new = s_mid + 0.16 * laplace(subst) - feeding + 0.04 * (1.0 - s_mid)
    a_new = a_mid + 0.08 * laplace(activ) + feeding - 0.1 * a_mid
    return (s_new, a_new)


def shade(values, material, color_table, alpha_table):
    table = jnp.concatenate([color_table, alpha_table[:, None, :]], axis=1)
    kinds = table.shape[0]
    bins = table.shape[2]
    place = jnp.clip(values, 0.0, 1.0) * (bins - 1)
    result = jnp.zeros((4,) + values.shape, jnp.float32)
    for node in range(bins):
        weight = jnp.maximum(0.0, 1.0 - jnp.abs(place - node))
        chosen = jnp.zeros((4,) + material.shape, jnp.float32)
        for kind in range(kinds):
            chosen = chosen + (material == kind).astype(jnp.float32)[None] * table[
                kind, :, node
            ].reshape((4,) + (1,) * material.ndim)
        result = result + weight[None] * chosen
    return result


def block_orders(assign, groups, per_owner, my_tile):
    share = per_owner // groups
    layout = assign.reshape(groups, per_owner)
    source = layout // per_owner
    local_block = layout % per_owner
    owned = (source == my_tile).astype(jnp.int32)
    ranking = jnp.cumsum(owned, axis=1) - owned
    slot_ids = jnp.arange(share, dtype=jnp.int32)
    picked = owned[:, None, :] * (ranking[:, None, :] == slot_ids[None, :, None]).astype(jnp.int32)
    send_order = jnp.sum(picked * local_block[:, None, :], axis=2).reshape(groups * share)
    arrivals = lax.dynamic_index_in_dim(source, my_tile, 0, keepdims=False)
    places = jnp.arange(per_owner, dtype=jnp.int32)
    earlier = (
        (arrivals[:, None] == arrivals[None, :]) & (places[None, :] < places[:, None])
    ).astype(jnp.int32)
    recv_order = arrivals * share + jnp.sum(earlier, axis=1)
    return (send_order, recv_order)


def pick_blocks(data, order, block_rows):
    lead = data.shape[:2]
    blocks = data.reshape(lead + (data.shape[2] // block_rows, block_rows, data.shape[3]))
    taken = jnp.take(blocks, order, axis=2)
    return taken.reshape(lead + (order.shape[0] * block_rows, data.shape[3]))


def front_weights(keep):
    running = jnp.cumprod(keep, axis=0)
    return (jnp.concatenate([jnp.ones_like(running[:1]), running[:-1]], axis=0), running[-1])


def local(u_field, v_field, brick_material, color_table, alpha_table, assign):
    depth, rows, width = u_field.shape
    fields = jnp.stack([u_field, v_field])
    for step in range(2):
        padded = extended(fields, (("tile", 2), ("dev", 1)), 1)
        subst, activ = react_diffuse(padded[0], padded[1])
        fields = jnp.stack([subst, activ])
    groups = lax.axis_size("tile")
    per_owner = rows // RB
    z_brick = (lax.axis_index("dev") * depth + jnp.arange(depth, dtype=jnp.int32)) // BK
    x_brick = (lax.axis_index("tile") * rows + jnp.arange(per_owner, dtype=jnp.int32) * RB) // BK
    y_brick = jnp.arange(width, dtype=jnp.int32) // BK
    material = jnp.take(
        jnp.take(jnp.take(brick_material, z_brick, axis=0), x_brick, axis=1), y_brick, axis=2
    )
    material = material.reshape(depth, per_owner, 1, width)
    rgba = shade(activ.reshape(depth, per_owner, RB, width), material, color_table, alpha_table)
    rgba = rgba.reshape(4, depth, rows, width).astype(jnp.bfloat16)
    send_order, recv_order = block_orders(assign, groups, per_owner, lax.axis_index("tile"))
    outgoing = pick_blocks(rgba, send_order, RB).reshape(4, depth, groups, rows // groups, width)
    arrived = lax.all_to_all(outgoing, "tile", split_axis=2, concat_axis=2, tiled=True).reshape(
        4, depth, rows, width
    )
    ordered = pick_blocks(arrived, recv_order, RB)
    columns = lax.all_to_all(ordered, "dev", split_axis=2, concat_axis=1, tiled=True)
    colour = columns[:3].astype(jnp.float32)
    alpha = columns[3].astype(jnp.float32)
    before, final = front_weights(1.0 - alpha)
    image = jnp.sum(colour * (alpha * before)[None], axis=1)
    return (subst, activ, image)


def solution(mesh):
    in_specs = (P("dev", "tile", None), P("dev", "tile", None), P(), P(), P(), P())
    out_specs = (P("dev", "tile", None), P("dev", "tile", None), P(None, ("tile", "dev"), None))
    return jax.shard_map(local, mesh=mesh, in_specs=in_specs, out_specs=out_specs, check_vma=False)
```

profile of v0, /device:TPU:1, one launch (start us, length us, event | category | flops | bytes accessed | tf_op | source)
XLA Modules:
  0.0 314.6 jit_solution(18213068044348100453)
XLA Ops:
  0.7 3.2 %stack.19 = f32[1,8,64,1024]{3,0,2,1:T(1,128)S(1)} reshape(f32[8,64,1024]{2,1,0:T(8,128)} %param.9) | data formatting | bytes 4194304 | tf_op jit(solution)/shard_map/stack | solution.py:94
  7.9 5.1 %collective-permute-start = (f32[2,8,1,1024]{3,0,2,1:T(2,128)S(1)}, f32[2,8,1,1024]{3,0,2,1:T(2,128)S(1)}, u32[]{:S(2)}, u32[]{:S(2)}) collective-permute-start(f32[2,8,1,1024]{3,0,2,1:T(2,128)S(1)} %get-tuple-element.90), channel_id=1, source_target_pairs={{0,32},{32,64},{64,96},{1,33},{33,65},{65,97},{2,34},{34,66},{66,9... | collective-permute-start | bytes 196616 | tf_op jit(solution)/shard_map/ppermute | solution.py:18
  17.3 9.1 %gather_fusion.2 = s32[1024,8,8]{2,1,0:T(8,128)} fusion(s32[8,8,16]{1,0,2:T(8,128)S(1)} %copy.74, s32[1024]{0:T(1024)S(1)} %broadcast_clamp_fusion), kind=kCustom, calls=%fused_computation.4 | custom fusion | bytes 528384 | tf_op jit(solution)/shard_map/jit(_take)/gather | solution.py:104
  26.4 8.9 %convert_bitcast_fusion.3 = (f32[8,8,1024]{1,0,2:T(8,128)}, f32[8,8,1024]{1,0,2:T(8,128)}, f32[8,8,1024]{1,0,2:T(8,128)}, f32[8,8,1024]{1,0,2:T(8,128)}) fusion(s32[1024,8,8]{2,1,0:T(8,128)} %gather_fusion.2, pred[1024]{0:T(1024)(128)(4,1)S(1)} %fusion.37), kind=kLoop, calls=%fused_computation.15 | loop fusion | flops 589824 | bytes 1311744 | tf_op jit(solution)/shard_map/convert_element_type | solution.py:54
  35.3 2.8 copy.78
  38.1 2.8 copy.77
  40.9 2.8 copy.76
  43.7 2.8 copy.75
  48.1 2.9 multiply_add_fusion.3
  58.2 3.3 %collective-permute-start.3 = (f32[2,1,66,1024]{3,0,2,1:T(2,128)S(1)}, f32[2,1,66,1024]{3,0,2,1:T(2,128)S(1)}, u32[]{:S(2)}, u32[]{:S(2)}) collective-permute-start(f32[2,1,66,1024]{3,0,2,1:T(2,128)S(1)} %get-tuple-element.83), channel_id=1, source_target_pairs={{1,0},{2,1},{3,2},{4,3},{5,4},{6,5},{7,6},{8,7},{9,8},{10,9},{11,1... | collective-permute-start | bytes 1622024 | tf_op jit(solution)/shard_map/ppermute | solution.py:20
  61.5 3.4 %collective-permute-start.2 = (f32[2,1,66,1024]{3,0,2,1:T(2,128)S(1)}, f32[2,1,66,1024]{3,0,2,1:T(2,128)S(1)}, u32[]{:S(2)}, u32[]{:S(2)}) collective-permute-start(f32[2,1,66,1024]{3,0,2,1:T(2,128)S(1)} %get-tuple-element.82), channel_id=1, source_target_pairs={{0,1},{1,2},{2,3},{3,4},{4,5},{5,6},{6,7},{7,8},{8,9},{9,10},{10,1... | collective-permute-start | bytes 1622024 | tf_op jit(solution)/shard_map/ppermute | solution.py:18
  67.0 2.8 collective-permute-done.3
  71.0 7.9 %pad_maximum_fusion.1 = f32[2,10,66,1024]{3,0,2,1:T(2,128)} fusion(f32[2,1,66,1024]{3,0,2,1:T(2,128)S(1)} %collective-permute-done.3, f32[2,8,1,1024]{3,0,2,1:T(2,128)S(1)} %collective-permute-done.1, f32[1,8,64,1024]{3,0,2,1:T(1,128)S(1)} %stack.19, f32[1,8,64,1024]{3,0,2,1:T(1,128)S(1)} %copy-done.3, f32[2,8,1,1024]{3,0,2,1:T(2,128)S(1)} %collective-permute-done, ...), kind=kLoop, calls=%fused_computation.8 | loop fusion | flops 6758400 | bytes 10813440 | tf_op jit(solution)/shard_map/concatenate | solution.py:16
  78.9 11.8 %fusion.171 = (f32[1,10,66,1024]{3,0,2,1:T(1,128)}, f32[1,10,66,1024]{3,0,2,1:T(1,128)}) fusion(f32[2,10,66,1024]{3,0,2,1:T(2,128)} %pad_maximum_fusion.1), kind=kLoop, calls=%fused_computation.445 | loop fusion | bytes 10813440 | tf_op jit(solution)/shard_map/slice | solution.py:97
  90.7 2.4 copy.102
  97.9 4.3 %fusion.7 = (f32[1,8,64,1024]{3,2,1,0:T(8,128)S(1)}, f32[1,8,64,1024]{3,2,1,0:T(8,128)S(1)}) fusion(f32[8,64,1024]{2,1,0:T(8,128)S(1)} %copy-done.7, f32[10,66,1024]{2,1,0:T(8,128)S(1)} %bitcast.99, f32[10,66,1024]{2,1,0:T(8,128)S(1)} %bitcast.101, f32[8,64,1024]{2,1,0:T(8,128)S(1)} %slice.459), kind=kLoop, calls=%fused_computation.37 | loop fusion | flops 15204352 | bytes 29360128 | tf_op jit(solution)/shard_map/stack | solution.py:98
  103.6 4.2 %collective-permute-start.4 = (f32[2,8,1,1024]{3,2,1,0:T(1,128)S(1)}, f32[2,8,1,1024]{3,2,1,0:T(1,128)S(1)}, u32[]{:S(2)}, u32[]{:S(2)}) collective-permute-start(f32[2,8,1,1024]{3,2,1,0:T(1,128)S(1)} %get-tuple-element.88), channel_id=1, source_target_pairs={{0,32},{32,64},{64,96},{1,33},{33,65},{65,97},{2,34},{34,66},{66,9... | collective-permute-start | bytes 196616 | tf_op jit(solution)/shard_map/ppermute | solution.py:18
  111.9 5.5 %collective-permute-start.6 = (f32[2,1,66,1024]{3,0,2,1:T(2,128)S(1)}, f32[2,1,66,1024]{3,0,2,1:T(2,128)S(1)}, u32[]{:S(2)}, u32[]{:S(2)}) collective-permute-start(f32[2,1,66,1024]{3,0,2,1:T(2,128)S(1)} %copy.68), channel_id=1, source_target_pairs={{0,1},{1,2},{2,3},{3,4},{4,5},{5,6},{6,7},{7,8},{8,9},{9,10},{10,1... | collective-permute-start | bytes 1622024 | tf_op jit(solution)/shard_map/ppermute | solution.py:18
  119.6 2.5 collective-permute-done.7
  126.3 6.1 %maximum_bitcast_fusion.15 = (f32[8,8,8,1024]{3,2,1,0:T(8,128)}, f32[8,64,1024]{2,1,0:T(8,128)S(1)}, f32[8,64,1024]{2,1,0:T(8,128)}) fusion(f32[8,64,1024]{2,1,0:T(8,128)S(1)} %slice.471, f32[10,66,1024]{2,1,0:T(8,128)S(1)} %get-tuple-element.75, f32[10,66,1024]{2,1,0:T(8,128)S(1)} %get-tuple-element.74, f32[8,64,1024]{2,1,0:T(8,128)S(1)} %slice.465), kind=kLoop, calls=%fused_computation.92 | loop fusion | flops 17825792 | bytes 31457280 | tf_op jit(solution)/shard_map/max | solution.py:51
  132.4 9.7 %maximum_bitcast_fusion.14 = (f32[8,8,8,1024]{3,2,1,0:T(8,128)S(1)}, f32[8,8,8,1024]{3,2,1,0:T(8,128)S(1)}, f32[8,8,8,1024]{3,2,1,0:T(8,128)}, f32[8,8,8,1024]{3...) fusion(f32[8,64,1024]{2,1,0:T(8,128)S(1)} %get-tuple-element.72), kind=kLoop, calls=%fused_computation.91 | loop fusion | flops 32505856 | bytes 33554432 | tf_op jit(solution)/shard_map/max | solution.py:51
  142.1 20.5 %add_convert_fusion = bf16[4,8,8,8,1024]{4,3,2,1,0:T(8,128)(2,1)} fusion(f32[4,8,8,1024]{3,2,1,0:T(8,128)} %multiply_add_fusion, f32[8,8,8,1024]{3,2,1,0:T(8,128)} %get-tuple-element.106, f32[4,8,8,1024]{3,2,1,0:T(8,128)} %get-tuple-element.121, f32[8,8,8,1024]{3,2,1,0:T(8,128)} %get-tuple-element.105, f32[4,8,8,1024]{3,2,1,0:T(8,128)} %get-tuple-element.120, ...), kind=kLoop, calls=%fused_computation.5 | loop fusion | flops 67108864 | bytes 54525952 | tf_op jit(solution)/shard_map/convert_element_type | solution.py:109
  162.6 5.0 %gather_fusion.3 = bf16[8,4,8,8,1024]{4,3,2,1,0:T(8,128)(2,1)} fusion(bf16[4,8,8,8,1024]{4,3,2,1,0:T(8,128)(2,1)} %add_convert_fusion, s32[1024]{0:T(1024)S(1)} %pad_clamp_fusion.1), kind=kCustom, calls=%fused_computation.clone | custom fusion | bytes 8388640 | tf_op jit(solution)/shard_map/jit(_take)/gather | solution.py:83
  167.5 2.7 select_bitcast_fusion.1
  170.9 2.4 copy.80
  173.3 5.2 %all-to-all-start = ((bf16[4,8,4,16,1024]{4,3,1,0,2:T(8,128)(2,1)}), bf16[4,8,4,16,1024]{4,3,1,0,2:T(8,128)(2,1)}, u32[]{:S(2)}, u32[]{:S(2)}) async-start(bf16[4,8,4,16,1024]{4,3,1,0,2:T(8,128)(2,1)} %copy.80), calls=%async_computation | async-start | bytes 8388608 | tf_op jit(solution)/shard_map/all_to_all | solution.py:112
  178.7 42.4 %all-to-all-done = bf16[4,8,4,16,1024]{4,3,1,0,2:T(8,128)(2,1)} async-done(((bf16[4,8,4,16,1024]{4,3,1,0,2:T(8,128)(2,1)}), bf16[4,8,4,16,1024]{4,3,1,0,2:T(8,128)(2,1)}, u32[]{:S(2)}, u32[]{:S(2)}) %all-to-all-start) | async-done | bytes 4194336 | tf_op jit(solution)/shard_map/all_to_all | solution.py:112
  221.1 5.0 %copy.81 = bf16[4,8,4,16,1024]{4,3,2,1,0:T(8,128)(2,1)} copy(bf16[4,8,4,16,1024]{4,3,1,0,2:T(8,128)(2,1)} %all-to-all-done) | data formatting | bytes 8388608 | tf_op jit(solution)/shard_map/all_to_all | solution.py:112
  226.1 4.9 %gather_fusion.4 = bf16[8,4,8,8,1024]{4,3,2,1,0:T(8,128)(2,1)} fusion(bf16[4,8,8,8,1024]{4,3,2,1,0:T(8,128)(2,1)} %bitcast.105, s32[1024]{0:T(1024)S(1)} %pad_clamp_fusion), kind=kCustom, calls=%fused_computation.1.clone | custom fusion | bytes 8388640 | tf_op jit(solution)/shard_map/jit(_take)/gather | solution.py:83
  231.0 3.7 %copy_bitcast_fusion = bf16[4,8,64,1024]{3,2,1,0:T(8,128)(2,1)S(1)} fusion(bf16[8,4,8,8,1024]{4,3,2,1,0:T(8,128)(2,1)} %gather_fusion.4, pred[8]{0:T(512)(128)(4,1)S(1)} %get-tuple-element.67), kind=kLoop, calls=%fused_computation.9 | loop fusion | flops 2097152 | bytes 8388616 | tf_op jit(solution)/shard_map/reshape | solution.py:84
  234.7 2.3 copy.83
  237.0 67.2 %all_to_all.20 = bf16[4,8,64,1024]{3,1,0,2:T(8,128)(2,1)S(1)} all-to-all(bf16[4,8,64,1024]{3,1,0,2:T(8,128)(2,1)S(1)} %copy.83), channel_id=1, replica_groups=mesh['tile'=4,'dev'=32] {'dev'}, dimensions={2} | all-to-all | bytes 8388608 | tf_op jit(solution)/shard_map/all_to_all | solution.py:116
  (131 shorter events, 47.2 us)
Async XLA Ops:
  0.6 15.2 %copy-start = (s32[4,4,16]{2,1,0:T(4,128)S(1)}, s32[4,4,16]{2,1,0:T(4,128)}, u32[]{:S(2)}) copy-start(s32[4,4,16]{2,1,0:T(4,128)} %param.10) | copy-start | bytes 3076
  0.6 3.2 %copy-start.10 = (f32[8,64,1024]{2,1,0:T(8,128)S(1)}, f32[8,64,1024]{2,1,0:T(8,128)}, u32[]{:S(2)}) copy-start(f32[8,64,1024]{2,1,0:T(8,128)} %param.8) | copy-start | bytes 6291460
  5.3 7.7 %copy-start.11 = (f32[4,3,16]{2,0,1:T(4,128)S(1)}, f32[4,3,16]{2,0,1:T(4,128)}, u32[]{:S(2)}) copy-start(f32[4,3,16]{2,0,1:T(4,128)} %param.11) | copy-start | bytes 2308
  5.3 7.7 %copy-start.12 = (f32[4,16]{1,0:T(4,128)S(1)}, f32[4,16]{1,0:T(4,128)}, u32[]{:S(2)}) copy-start(f32[4,16]{1,0:T(4,128)} %param.12) | copy-start | bytes 772
  5.3 10.4 %copy-start.25 = (s32[32]{0:T(128)S(1)}, s32[32]{0:T(128)}, u32[]{:S(2)}) copy-start(s32[32]{0:T(128)} %param.13) | copy-start | bytes 388
  6.6 49.5 %collective-permute-start.1 = (f32[2,8,1,1024]{3,0,2,1:T(2,128)S(1)}, f32[2,8,1,1024]{3,0,2,1:T(2,128)S(1)}, u32[]{:S(2)}, u32[]{:S(2)}) collective-permute-start(f32[2,8,1,1024]{3,0,2,1:T(2,128)S(1)} %get-tuple-element.91), channel_id=1, source_target_pairs={{32,0},{64,32},{96,64},{33,1},{65,33},{97,65},{34,2},{66,34},{98,6... | collective-permute-start | bytes 196616 | tf_op jit(solution)/shard_map/ppermute | solution.py:20
  7.9 48.3 %collective-permute-start = (f32[2,8,1,1024]{3,0,2,1:T(2,128)S(1)}, f32[2,8,1,1024]{3,0,2,1:T(2,128)S(1)}, u32[]{:S(2)}, u32[]{:S(2)}) collective-permute-start(f32[2,8,1,1024]{3,0,2,1:T(2,128)S(1)} %get-tuple-element.90), channel_id=1, source_target_pairs={{0,32},{32,64},{64,96},{1,33},{33,65},{65,97},{2,34},{34,66},{66,9... | collective-permute-start | bytes 196616 | tf_op jit(solution)/shard_map/ppermute | solution.py:18
  48.0 3.0 copy-start.13
  48.0 3.0 copy-start.14
  48.0 3.0 copy-start.15
  48.0 3.0 copy-start.16
  48.0 3.0 copy-start.17
  48.0 3.0 copy-start.18
  48.0 3.0 copy-start.19
  48.0 3.0 copy-start.20
  48.0 3.0 copy-start.21
  48.0 3.0 copy-start.22
  48.1 3.0 copy-start.23
  48.1 3.0 copy-start.24
  58.2 11.6 %collective-permute-start.3 = (f32[2,1,66,1024]{3,0,2,1:T(2,128)S(1)}, f32[2,1,66,1024]{3,0,2,1:T(2,128)S(1)}, u32[]{:S(2)}, u32[]{:S(2)}) collective-permute-start(f32[2,1,66,1024]{3,0,2,1:T(2,128)S(1)} %get-tuple-element.83), channel_id=1, source_target_pairs={{1,0},{2,1},{3,2},{4,3},{5,4},{6,5},{7,6},{8,7},{9,8},{10,9},{11,1... | collective-permute-start | bytes 1622024 | tf_op jit(solution)/shard_map/ppermute | solution.py:20
  61.5 9.5 %collective-permute-start.2 = (f32[2,1,66,1024]{3,0,2,1:T(2,128)S(1)}, f32[2,1,66,1024]{3,0,2,1:T(2,128)S(1)}, u32[]{:S(2)}, u32[]{:S(2)}) collective-permute-start(f32[2,1,66,1024]{3,0,2,1:T(2,128)S(1)} %get-tuple-element.82), channel_id=1, source_target_pairs={{0,1},{1,2},{2,3},{3,4},{4,5},{5,6},{6,7},{7,8},{8,9},{9,10},{10,1... | collective-permute-start | bytes 1622024 | tf_op jit(solution)/shard_map/ppermute | solution.py:18
  64.9 6.1 %copy-start.3 = (f32[1,8,64,1024]{3,0,2,1:T(1,128)S(1)}, f32[1,8,64,1024]{3,0,2,1:T(1,128)}, u32[]{:S(2)}) copy-start(f32[1,8,64,1024]{3,0,2,1:T(1,128)} %copy-done.2) | copy-start | bytes 6291460
  93.1 2.5 copy-start.6
  102.3 5.5 %collective-permute-start.5 = (f32[2,8,1,1024]{3,2,1,0:T(1,128)S(1)}, f32[2,8,1,1024]{3,2,1,0:T(1,128)S(1)}, u32[]{:S(2)}, u32[]{:S(2)}) collective-permute-start(f32[2,8,1,1024]{3,2,1,0:T(1,128)S(1)} %get-tuple-element.89), channel_id=1, source_target_pairs={{32,0},{64,32},{96,64},{33,1},{65,33},{97,65},{34,2},{66,34},{98,6... | collective-permute-start | bytes 196616 | tf_op jit(solution)/shard_map/ppermute | solution.py:20
  103.6 5.3 %collective-permute-start.4 = (f32[2,8,1,1024]{3,2,1,0:T(1,128)S(1)}, f32[2,8,1,1024]{3,2,1,0:T(1,128)S(1)}, u32[]{:S(2)}, u32[]{:S(2)}) collective-permute-start(f32[2,8,1,1024]{3,2,1,0:T(1,128)S(1)} %get-tuple-element.88), channel_id=1, source_target_pairs={{0,32},{32,64},{64,96},{1,33},{33,65},{65,97},{2,34},{34,66},{66,9... | collective-permute-start | bytes 196616 | tf_op jit(solution)/shard_map/ppermute | solution.py:18
  109.6 12.6 %collective-permute-start.7 = (f32[2,1,66,1024]{3,0,2,1:T(2,128)S(1)}, f32[2,1,66,1024]{3,0,2,1:T(2,128)S(1)}, u32[]{:S(2)}, u32[]{:S(2)}) collective-permute-start(f32[2,1,66,1024]{3,0,2,1:T(2,128)S(1)} %copy.69), channel_id=1, source_target_pairs={{1,0},{2,1},{3,2},{4,3},{5,4},{6,5},{7,6},{8,7},{9,8},{10,9},{11,1... | collective-permute-start | bytes 1622024 | tf_op jit(solution)/shard_map/ppermute | solution.py:20
  111.9 11.8 %collective-permute-start.6 = (f32[2,1,66,1024]{3,0,2,1:T(2,128)S(1)}, f32[2,1,66,1024]{3,0,2,1:T(2,128)S(1)}, u32[]{:S(2)}, u32[]{:S(2)}) collective-permute-start(f32[2,1,66,1024]{3,0,2,1:T(2,128)S(1)} %copy.68), channel_id=1, source_target_pairs={{0,1},{1,2},{2,3},{3,4},{4,5},{5,6},{6,7},{7,8},{8,9},{9,10},{10,1... | collective-permute-start | bytes 1622024 | tf_op jit(solution)/shard_map/ppermute | solution.py:18
  132.4 9.7 %copy-start.9 = (f32[8,64,1024]{2,1,0:T(8,128)}, f32[8,64,1024]{2,1,0:T(8,128)S(1)}, u32[]{:S(2)}) copy-start(f32[8,64,1024]{2,1,0:T(8,128)S(1)} %get-tuple-element.72) | copy-start | bytes 6291460
  173.3 47.8 %all-to-all-start = ((bf16[4,8,4,16,1024]{4,3,1,0,2:T(8,128)(2,1)}), bf16[4,8,4,16,1024]{4,3,1,0,2:T(8,128)(2,1)}, u32[]{:S(2)}, u32[]{:S(2)}) async-start(bf16[4,8,4,16,1024]{4,3,1,0,2:T(8,128)(2,1)} %copy.80), calls=%async_computation | async-start | bytes 8388608 | tf_op jit(solution)/shard_map/all_to_all | solution.py:112
  304.8 2.6 copy-start.4
  310.2 2.3 copy-start.5
  311.4 2.7 copy-start.1
  (3 other events, 5.2 us)
where the time goes:
time: 318 us; the launch traced here: 315 us
  other arithmetic  90.2 us (28%)
  local copies, waits for them, and re-layouts  72.9 us (23%)
  blocking collectives  67.2 us (21%)
  waiting for transfers between devices  51.4 us (16%)
  starting transfers between devices  31.1 us (10%)
    all_to_all x1, blocking collectives, local(): lax.all_to_all(ordered, 'dev', split_axis=2, concat_axis=1, tiled=True)  67.2 us
    all_to_all x1, waiting for transfers between devices, local(): lax.all_to_all(outgoing, 'tile', split_axis=2, concat_axis=2, tiled=True)  42.4 us
    convert_element_type x1, other arithmetic, local(): rgba = rgba.reshape(4, depth, rows, width).astype(jnp.bfloat16)  20.5 us
    ppermute x4, starting transfers between devices, extended(): lax.ppermute(tail, axis, [(i, (i + 1) % count) for i in range(ends)])  18.2 us
    max x2, other arithmetic, shade(): weight = jnp.maximum(0.0, 1.0 - jnp.abs(place - node))  15.8 us
    add x6, other arithmetic, shade(): chosen + (material == kind).astype(jnp.float32)[None] * table[kind, :, no...  12.8 us
    slice x1, local copies, waits for them, and re-layouts, local(): subst, activ = react_diffuse(padded[0], padded[1])  11.8 us
    convert_element_type x4, local copies, waits for them, and re-layouts, shade(): (material == kind).astype(jnp.float32)[None]  11.2 us
  transfers between devices with their start and end apart: 9, of which 6 were waited for; matrix products, arithmetic and copies ran while one was open for 15% of the time, Pallas kernels for 0%

commit v1 on v0

v1 whole, which is shorter than its diff:
```python
import jax
import jax.numpy as jnp
from jax import lax
from jax.experimental import pallas as pl
from jax.experimental.pallas import tpu as pltpu
from jax.sharding import PartitionSpec as P

MESH = pl.DeviceIdType.MESH
I16 = jnp.int16
I32 = jnp.int32
F32 = jnp.float32
DZ, NR, NY = 8, 64, 1024
LT = 8
ROW0 = 8
STEPS, SHIFT = 65534.0, 32767.0
TOPS = (0.32, 0.32, 0.32, 0.16)


def enc(x, top):
    return jnp.round(x * (STEPS / top) - SHIFT).astype(I32).astype(I16)


def dec(x, top):
    return (x.astype(I32).astype(F32) + SHIFT) * (top / STEPS)


def gather(tab, idx):
    return jnp.take_along_axis(tab, idx, axis=1, mode="promise_in_bounds")


def cells(ref, f, j, z0, nz, r0):
    return ref[f, j, pl.ds(z0, nz), pl.ds(r0, 8), :]


def neighbours(ref, f, j, z0, nz, r0, c, lanes):
    depth = cells(ref, f, j, z0 - 1, nz, r0) + cells(ref, f, j, z0 + 1, nz, r0)
    row = cells(ref, f, j, z0, nz, r0 - 1) + cells(ref, f, j, z0, nz, r0 + 1)
    left = pltpu.roll(jnp.where(lanes == 127, cells(ref, f, j - 1, z0, nz, r0), c), 1, 2)
    right = pltpu.roll(jnp.where(lanes == 0, cells(ref, f, j + 1, z0, nz, r0), c), 127, 2)
    return depth + row + (left + right)


def advance(ref, j, z0, nz, r0):
    lanes = lax.broadcasted_iota(I32, (nz, 8, 128), 2)
    u, v = (cells(ref, f, j, z0, nz, r0) for f in range(2))
    su = neighbours(ref, 0, j, z0, nz, r0, u, lanes)
    sv = neighbours(ref, 1, j, z0, nz, r0, v, lanes)
    r = u * v * v
    return 0.16 * su - r + 0.04, 0.08 * sv + (0.42 * v + r)


def kernel(bricks, assign, u, v, color, alpha, u_out, v_out, image, a, b, o, coded, zbuf, tabs, part, slots,
           away, came, pair, got, own, pick, stage, lines, isem, osem, hs, hr, cs, cr, ps, pr, fs, fr, lsem):
    t, d = lax.axis_index("tile"), lax.axis_index("dev")
    nt, nd = lax.axis_size("tile"), lax.axis_size("dev")
    tu, td = lax.rem(t + 1, nt), lax.rem(t + nt - 1, nt)
    du, dd = lax.rem(d + 1, nd), lax.rem(d + nd - 1, nd)
    z, y, core = d // 8, lax.rem(d // 2, 4), lax.rem(d, 2)
    fields, outs = (u, v), (u_out, v_out)
    inz = (d > 0, d < nd - 1)
    inx = (t > 0, t < nt - 1)

    def fetch(f, j):
        return pltpu.make_async_copy(
            fields[f].at[:, :, pl.ds(j * 128, 128)], a.at[f, j + 1, pl.ds(2, DZ), pl.ds(ROW0, NR), :], isem.at[f, j])

    for j in range(LT):
        for f in range(2):
            fetch(f, j).start()

    barrier = pltpu.get_barrier_semaphore()

    def greet(who):
        pl.semaphore_signal(barrier, inc=1, device_id=who, device_id_type=MESH)

    around = [(tt, d2) for tt in (td, t, tu) for d2 in (dd, d, du)]
    around.pop(4)
    for who in around:
        greet(who)

    def chip(k):
        return lax.rem(z + k // 4, 4) * 8 + lax.rem(y + lax.rem(k, 4), 4) * 2 + core

    @pl.loop(1, 16)
    def _(k):
        greet((t, chip(k)))

    rq = lax.rem(d, 4)

    @pl.loop(0, 8)
    def _(k):
        who_t, who_d = lax.rem(t + k // 2, nt), t * 8 + rq * 2 + lax.rem(k, 2)

        @pl.when(jnp.logical_not((who_t == t) & (who_d == d)))
        def _():
            greet((who_t, who_d))

    lanes = lax.broadcasted_iota(I32, (8, 128), 1)
    kf = lax.rem(lanes, 16).astype(F32)
    for j in range(LT):
        for cc in range(4):
            rows = []
            for half in range(2):
                m = bricks[d * DZ // 64, t * NR // 64, 2 * j + half]
                row = color[m, cc] if cc < 3 else alpha[m, 0]
                rows.append(jnp.broadcast_to(row[None], (8, 128)))
            nodes = jnp.where(lanes < 16, rows[0], pltpu.roll(rows[1], 16, 1))
            slope = jnp.where(lax.rem(lanes, 16) == 15, 0.0, pltpu.roll(nodes, 127, 1) - nodes)
            tabs[j, 2 * cc] = nodes - kf * slope
            tabs[j, 2 * cc + 1] = slope

    order = []
    for g in range(4):
        seen = jnp.int32(0)
        found = [jnp.int32(0), jnp.int32(0)]
        for p in range(8):
            w = assign[8 * g + p]
            mine = (w // 8 == t).astype(I32)
            for h in range(2):
                found[h] = found[h] + mine * (seen == h).astype(I32) * lax.rem(w, 8)
            seen = seen + mine
        order += found

    for ref, nz, nr in ((a, DZ + 4, NR + 16), (b, DZ + 2, NR + 8)):
        for f in range(2):
            for j in (0, LT + 1):

                @pl.loop(0, nz)
                def _(k):
                    ref[f, j, k] = jnp.zeros((nr, 128), F32)

    for j in range(LT):
        for f in range(2):
            fetch(f, j).wait()

        @pl.loop(0, 2)
        def _(f):
            for side, z0 in ((0, DZ), (1, 2)):
                for k in range(2):
                    coded[side, j, f, k] = enc(a[f, j + 1, z0 + k, pl.ds(ROW0, NR), :], 1.0)

    pl.semaphore_wait(barrier, 8 + 15 + 8 - ((z == t) & (rq == y)).astype(I32))

    copies = []

    def send(src, dst, who):
        n = len(copies)
        c = pltpu.make_async_remote_copy(src_ref=src, dst_ref=dst, send_sem=hs.at[n], recv_sem=hr.at[n], device_id=who, device_id_type=MESH)
        c.start()
        copies.append(c)

    inner = pl.ds(1, LT)
    for k in range(ZCH):
        js = pl.ds(k * (LT // ZCH), LT // ZCH)
        for side, who in ((0, du), (1, dd)):
            send(coded.at[side, js], zbuf.at[side, js], (t, who))
        if k == 0:
            depth = pl.ds(2, DZ)
            send(a.at[:, inner, depth, pl.ds(ROW0 + NR - 2, 2), :], a.at[:, inner, depth, pl.ds(ROW0 - 2, 2), :], (tu, d))
            send(a.at[:, inner, depth, pl.ds(ROW0, 2), :], a.at[:, inner, depth, pl.ds(ROW0 + NR, 2), :], (td, d))
            for z0, z1, wz in ((DZ + 1, 1, du), (2, DZ + 2, dd)):
                for r0, r1, wx in ((ROW0 + NR - 1, ROW0 - 1, tu), (ROW0, ROW0 + NR, td)):
                    send(a.at[:, inner, z0, pl.ds(r0, 1), :], a.at[:, inner, z1, pl.ds(r1, 1), :], (wx, wz))

    for c in copies[2:8]:
        c.wait()
    for s in range(2):

        @pl.when(jnp.logical_not(inx[s]))
        def _():
            @pl.loop(1, LT + 1)
            def _(j):
                for f in range(2):
                    for k in range(1, DZ + 3):
                        a[f, j, k, pl.ds(ROW0 + NR if s else ROW0 - 2, 2), :] = jnp.zeros((2, 128), F32)

    def first(z0, nz):
        def body(i, carry):
            j, r = 1 + i // 9, lax.rem(i, 9)
            nu, nv = advance(a, j, z0, nz, ROW0 - 1 + 8 * r)
            b[0, j, pl.ds(z0 - 1, nz), pl.ds(8 * r, 8), :] = nu
            b[1, j, pl.ds(z0 - 1, nz), pl.ds(8 * r, 8), :] = nv
            return carry

        lax.fori_loop(0, LT * 9, body, 0, unroll=9)

    def clear_rows(z0, nz):
        for s in range(2):

            @pl.when(jnp.logical_not(inx[s]))
            def _():
                @pl.loop(1, LT + 1)
                def _(j):
                    for f in range(2):
                        for k in range(z0, z0 + nz):
                            b[f, j, k, pl.ds((NR + 1) * s, 1), :] = jnp.zeros((1, 128), F32)

    def second(z0, nz):
        def body(i, carry):
            j, r = i // 8, pl.multiple_of(lax.rem(i, 8) * 8, 8)
            nu, nv = advance(b, j + 1, z0, nz, r + 1)
            o[0, j, pl.ds(z0 - 1, nz), pl.ds(r, 8), :] = nu
            o[1, j, pl.ds(z0 - 1, nz), pl.ds(r, 8), :] = nv
            return carry

        lax.fori_loop(0, LT * 8, body, 0, unroll=8)

    offset = jnp.where(lanes >= 64, 16, 0)

    def shade(j, z0, nz, r):
        keep, total = None, [None] * 3
        for k in range(z0, z0 + nz):
            p = jnp.clip(o[1, j, k, pl.ds(r, 8), :] * 15.0, 0.0, 15.0)
            idx = p.astype(I32) + offset
            vals = []
            for cc in range(4):
                x = gather(tabs[j, 2 * cc], idx) + gather(tabs[j, 2 * cc + 1], idx) * p
                vals.append(x.astype(jnp.bfloat16).astype(F32))
            w = vals[3] if keep is None else vals[3] * keep
            keep = 1.0 - w if keep is None else keep - w
            for cc in range(3):
                x = vals[cc] * w
                total[cc] = x if total[cc] is None else total[cc] + x
        return total, keep

    first(3, 6)
    clear_rows(2, 6)
    second(3, 4)

    def middle(i, carry):
        j, r = i // 8, lax.rem(i, 8)
        total, keep = shade(j, 2, 4, pl.multiple_of(r * 8, 8))
        for cc in range(3):
            part[r, j, cc] = total[cc]
        part[r, j, 3] = keep
        return carry

    lax.fori_loop(0, LT * 8, middle, 0, unroll=4)

    for c in copies[:2] + copies[8:]:
        c.wait()

    @pl.loop(0, LT)
    def _(j):
        for s in range(2):
            for f in range(2):
                for k in range(2):
                    x = dec(zbuf[s, j, f, k], 1.0)
                    a[f, j + 1, (DZ + 2) * s + k, pl.ds(ROW0, NR), :] = jnp.where(inz[s], x, 0.0)

    for s in range(2):

        @pl.when(jnp.logical_not(inz[s]))
        def _():
            @pl.loop(1, LT + 1)
            def _(j):
                for f in range(2):
                    for r in (ROW0 - 1, ROW0 + NR):
                        a[f, j, (DZ + 1) * s + 1, pl.ds(r, 1), :] = jnp.zeros((1, 128), F32)

    first(1, 2)
    first(9, 2)
    clear_rows(0, 2)
    clear_rows(8, 2)
    for s in range(2):

        @pl.when(jnp.logical_not(inz[s]))
        def _():
            @pl.loop(1, LT + 1)
            def _(j):
                for f in range(2):
                    b[f, j, (DZ + 1) * s] = jnp.zeros((NR + 8, 128), F32)

    second(1, 2)
    second(7, 2)

    def emit(f, j):
        return pltpu.make_async_copy(o.at[f, j], outs[f].at[:, :, pl.ds(j * 128, 128)], osem.at[f, j])

    for j in range(LT):
        for f in range(2):
            emit(f, j).start()

    def ends(i, carry):
        j, r = i // 8, lax.rem(i, 8)
        front, keep = shade(j, 0, 2, pl.multiple_of(r * 8, 8))
        back, last = shade(j, 6, 2, pl.multiple_of(r * 8, 8))
        mid = part[r, j, 3]
        for cc in range(3):
            part[r, j, cc] = front[cc] + keep * (part[r, j, cc] + mid * back[cc])
        part[r, j, 3] = 1.0 - keep * mid * last
        return carry

    lax.fori_loop(0, LT * 8, ends, 0, unroll=4)

    for i in range(8):
        for j in range(LT):
            for cc in range(4):
                slots[j // 4, i // 2, cc, pl.ds(2 * (j % 4) + i % 2, 8, stride=8), :] = part[order[i], j, cc]

    def pack(i, carry):
        g, q = i // 4, lax.rem(i, 4)
        for cc in range(4):
            away[g, q, cc] = enc(slots[1 - core, g, cc, pl.ds(pl.multiple_of(16 * q, 16), 16), :], TOPS[cc])
        return carry

    lax.fori_loop(0, 16, pack, 0, unroll=2)
    swap = pltpu.make_async_remote_copy(src_ref=away, dst_ref=came, send_sem=cs, recv_sem=cr, device_id=(t, d + 1 - 2 * core), device_id_type=MESH)
    swap.start()
    swap.wait()

    def join(i, carry):
        g, q = i // 4, lax.rem(i, 4)
        rows = pl.ds(pl.multiple_of(16 * q, 16), 16)
        x = [slots[core, g, cc, rows, :] for cc in range(4)]
        w = [dec(came[g, q, cc], TOPS[cc]) for cc in range(4)]
        ahead = core == 0
        clear = 1.0 - jnp.where(ahead, x[3], w[3])
        for cc in range(4):
            f, s = jnp.where(ahead, x[cc], w[cc]), jnp.where(ahead, w[cc], x[cc])
            pair[g, q, cc] = enc(f + clear * s, 2 * TOPS[cc])
        return carry

    lax.fori_loop(0, 16, join, 0, unroll=2)

    here = z * 4 + y

    def share(k):
        to_z, to_y = lax.rem(z + k // 4, 4), lax.rem(y + lax.rem(k, 4), 4)
        return pltpu.make_async_remote_copy(
            src_ref=pair.at[to_z, to_y], dst_ref=got.at[here], send_sem=ps.at[k], recv_sem=pr.at[k],
            device_id=(t, to_z * 8 + to_y * 2 + core), device_id_type=MESH)

    @pl.loop(1, 16)
    def _(k):
        share(k).start()

    keep_own = pltpu.make_async_copy(pair.at[z, y], got.at[here], lsem)
    keep_own.start()
    keep_own.wait()

    @pl.loop(1, 16)
    def _(k):
        share(k).wait()

    def fold(s, carry):
        keep, total = carry
        x = [dec(got[s, cc], 2 * TOPS[cc]) for cc in range(4)]
        total = tuple(total[cc] + x[cc] * keep for cc in range(3))
        return keep - keep * x[3], total

    zero = jnp.zeros((16, 128), F32)
    _, total = lax.fori_loop(0, 16, fold, (zero + 1.0, (zero, zero, zero)), unroll=4)
    for cc in range(3):
        own[cc] = total[cc]
        for h in range(2):
            pick[h, cc] = own[cc, pl.ds(h, 8, stride=2), :]

    for p in range(8):
        w = assign[8 * z + p] // 8
        s = jnp.int32(0)
        for q in range(p):
            s = s + (assign[8 * z + q] // 8 == w).astype(I32)
        s = jnp.minimum(s, 1)
        for cc in range(3):
            stage[p, cc] = pick[s, cc]

    def spread(k):
        p = lax.rem(k + d // 4, 8)
        return p, (z == t) & (4 * p + y == d), pltpu.make_async_remote_copy(
            src_ref=stage.at[p], dst_ref=lines.at[t, core], send_sem=fs.at[k], recv_sem=fr.at[t, core],
            device_id=(z, 4 * p + y), device_id_type=MESH)

    @pl.loop(0, 8)
    def _(k):
        p, self_, c = spread(k)

        @pl.when(jnp.logical_not(self_))
        def _():
            c.start()

        @pl.when(self_)
        def _():
            pltpu.make_async_copy(stage.at[p], lines.at[t, core], fr.at[t, core]).start()

    @pl.loop(0, 8)
    def _(k):
        p, self_, c = spread(k)

        @pl.when(jnp.logical_not(self_))
        def _():
            c.wait_send()

    for k in range(8):
        pltpu.make_async_copy(stage.at[0], lines.at[k // 2, k % 2], fr.at[k // 2, k % 2]).wait()

    w = assign[8 * t + d // 4] // 8
    for half in range(2):
        for cc in range(3):
            x = lines[w, half, cc]
            for r in range(2):
                for l in range(4):
                    image[cc, r : r + 1, pl.ds((4 * half + l) * 128, 128)] = x[4 * r + l : 4 * r + l + 1]

    for j in range(LT):
        for f in range(2):
            emit(f, j).wait()


ZCH = 4


def local(u, v, bricks, color, alpha, assign):
    hbm = pl.BlockSpec(memory_space=pltpu.HBM)
    smem = pl.BlockSpec(memory_space=pltpu.SMEM)
    vmem = pl.BlockSpec(memory_space=pltpu.VMEM)
    color = jnp.pad(color, ((0, 0), (0, 0), (0, 112)))
    alpha = jnp.pad(alpha[:, None], ((0, 0), (0, 0), (0, 112)))
    dma = pltpu.SemaphoreType.DMA
    return pl.pallas_call(
        kernel,
        out_shape=(
            jax.ShapeDtypeStruct((DZ, NR, NY), F32),
            jax.ShapeDtypeStruct((DZ, NR, NY), F32),
            jax.ShapeDtypeStruct((3, 2, NY), F32),
        ),
        in_specs=[smem, smem, hbm, hbm, vmem, vmem],
        out_specs=(hbm, hbm, vmem),
        scratch_shapes=[
            pltpu.VMEM((2, LT + 2, DZ + 4, NR + 16, 128), F32),
            pltpu.VMEM((2, LT + 2, DZ + 2, NR + 8, 128), F32),
            pltpu.VMEM((2, LT, DZ, NR, 128), F32),
            pltpu.VMEM((2, LT, 2, 2, NR, 128), I16),
            pltpu.VMEM((2, LT, 2, 2, NR, 128), I16),
            pltpu.VMEM((LT, 8, 8, 128), F32),
            pltpu.VMEM((NR // 8, LT, 4, 8, 128), F32),
            pltpu.VMEM((2, 4, 4, NR, 128), F32),
            pltpu.VMEM((4, 4, 4, 16, 128), I16),
            pltpu.VMEM((4, 4, 4, 16, 128), I16),
            pltpu.VMEM((4, 4, 4, 16, 128), I16),
            pltpu.VMEM((16, 4, 16, 128), I16),
            pltpu.VMEM((3, 16, 128), F32),
            pltpu.VMEM((2, 3, 8, 128), F32),
            pltpu.VMEM((8, 3, 8, 128), F32),
            pltpu.VMEM((4, 2, 3, 8, 128), F32),
            dma((2, LT)), dma((2, LT)),
            dma((6 + 2 * ZCH,)), dma((6 + 2 * ZCH,)),
            dma, dma,
            dma((16,)), dma((16,)),
            dma((8,)), dma((4, 2)),
            dma,
        ],
        compiler_params=pltpu.CompilerParams(collective_id=0, has_side_effects=True, vmem_limit_bytes=48 << 20),
        name="reaction_render",
    )(bricks, assign, u, v, color, alpha)


def solution(mesh):
    in_specs = (P("dev", "tile", None), P("dev", "tile", None), P(), P(), P(), P())
    out_specs = (P("dev", "tile", None), P("dev", "tile", None), P(None, ("tile", "dev"), None))
    return jax.shard_map(local, mesh=mesh, in_specs=in_specs, out_specs=out_specs, check_vma=False)
```

time: 318 us -> 60.6 us (0.19)
  the two profiles are of different devices: /device:TPU:1 before, /device:TPU:8 now
where the time goes in v1:
time: 60.6 us; the launch traced here: 60.4 us
  Pallas kernels  53.8 us (89%)
  local copies, waits for them, and re-layouts  5.99 us (10%)
  between operations  0.65 us (1%)
    pallas_call x1, Pallas kernels, local(): pl.pallas_call(kernel, out_shape=(jax.ShapeDtypeStruct((DZ, NR, NY), F32)...  53.8 us
    unnamed x8, local copies, waits for them, and re-layouts  5.29 us

profile of v1, /device:TPU:8, one launch (start us, length us, event | category | flops | bytes accessed | tf_op | source)
XLA Modules:
  0.0 60.4 jit_solution(11800923210955951461)
XLA Ops:
  0.6 0.7 %pad.9.alpha = f32[4,1,128]{2,1,0:T(1,128)S(1)} pad(f32[4,1,16]{2,1,0:T(1,128)} %bitcast.3, f32[]{:T(128)} %constant.2.clone.1), padding=0_0x0_0x0_112 | pad | bytes 2308 | tf_op jit(solution)/shard_map/jit(_pad)/pad | solution.py:418
  1.3 0.7 %copy.9 = f32[4,3,16]{2,1,0:T(4,128)S(1)} copy(f32[4,3,16]{2,0,1:T(4,128)} %param.9) | data formatting | bytes 1536 | tf_op args[3]
  2.0 0.0 copy-start
  2.0 0.7 %copy-done = s32[4,4,16]{2,1,0:T(4,128)S(1)} copy-done((s32[4,4,16]{2,1,0:T(4,128)S(1)}, s32[4,4,16]{2,1,0:T(4,128)}, u32[]{:S(2)}) %copy-start) | copy-done | bytes 1048
  2.7 0.0 copy-start.1
  2.7 0.7 %copy-done.1 = s32[32]{0:T(128)S(1)} copy-done((s32[32]{0:T(128)S(1)}, s32[32]{0:T(128)}, u32[]{:S(2)}) %copy-start.1) | copy-done | bytes 152
  3.4 53.8 %reaction_render.1 = (f32[8,64,1024]{2,1,0:T(8,128)S(1)}, f32[8,64,1024]{2,1,0:T(8,128)S(1)}, f32[3,2,1024]{2,1,0:T(2,128)S(1)}) custom-call(s32[4,4,16]{2,1,0:T(4,128)S(1)} %copy-done, s32[32]{0:T(128)S(1)} %copy-done.1, f32[8,64,1024]{2,1,0:T(8,128)} %u.1, f32[8,64,1024]{2,1,0:T(8,128)} %v.1, f32[4,3,128]{2,1,0:T(4,128)S(1)} %pad.8.color, ...), custom_call_target="tpu_custom_call" | custom-call | tf_op jit(solution)/shard_map/reaction_render/pallas_call | solution.py:420
  57.2 1.3 %copy.14 = f32[8,64,1024]{2,1,0:T(8,128)} copy(f32[8,64,1024]{2,1,0:T(8,128)S(1)} %get-tuple-element.6) | data formatting | bytes 4194304
  58.5 1.3 %copy.15 = f32[8,64,1024]{2,1,0:T(8,128)} copy(f32[8,64,1024]{2,1,0:T(8,128)S(1)} %get-tuple-element.7) | data formatting | bytes 4194304
  59.8 0.6 %copy.16 = f32[3,2,1024]{2,1,0:T(2,128)} copy(f32[3,2,1024]{2,1,0:T(2,128)S(1)} %get-tuple-element.8) | data formatting | bytes 49152
  (1 shorter events, 0.0 us)
Async XLA Ops:
  2.0 0.7 %copy-start = (s32[4,4,16]{2,1,0:T(4,128)S(1)}, s32[4,4,16]{2,1,0:T(4,128)}, u32[]{:S(2)}) copy-start(s32[4,4,16]{2,1,0:T(4,128)} %bricks.1) | copy-start | bytes 3076
  2.7 0.7 %copy-start.1 = (s32[32]{0:T(128)S(1)}, s32[32]{0:T(128)}, u32[]{:S(2)}) copy-start(s32[32]{0:T(128)} %assign.1) | copy-start | bytes 388

commit v2 on v1

v2 whole, which is shorter than its diff:
```python
import jax
import jax.numpy as jnp
from jax import lax
from jax.experimental import pallas as pl
from jax.experimental.pallas import tpu as pltpu
from jax.sharding import PartitionSpec as P

MESH = pl.DeviceIdType.MESH
I16 = jnp.int16
I32 = jnp.int32
F32 = jnp.float32
DZ, NR, NY = 8, 64, 1024
LT = 8
ROW0 = 8
CU, AU = 2.0**-14, 2.0**-21
STEPS, SHIFT = 65534.0, 32767.0
TOPS = (0.32 / CU, 0.32 / CU, 0.32 / CU, 0.16)
CH = 4


def enc(x, top):
    return jnp.round(x * (STEPS / top) - SHIFT).astype(I32).astype(I16)


def dec(x, top):
    return (x.astype(I32).astype(F32) + SHIFT) * (top / STEPS)


def gather(tab, idx):
    return jnp.take_along_axis(tab, idx, axis=1, mode="promise_in_bounds")


def cells(ref, f, j, z0, nz, r0):
    return ref[f, j, pl.ds(z0, nz), pl.ds(r0, 8), :]


def neighbours(ref, f, j, z0, nz, r0, c, lanes):
    depth = cells(ref, f, j, z0 - 1, nz, r0) + cells(ref, f, j, z0 + 1, nz, r0)
    row = cells(ref, f, j, z0, nz, r0 - 1) + cells(ref, f, j, z0, nz, r0 + 1)
    left = pltpu.roll(jnp.where(lanes == 127, cells(ref, f, j - 1, z0, nz, r0), c), 1, 2)
    right = pltpu.roll(jnp.where(lanes == 0, cells(ref, f, j + 1, z0, nz, r0), c), 127, 2)
    return depth + row + (left + right)


def next_u(ref, j, z0, nz, r0, u, v, lanes):
    return 0.16 * neighbours(ref, 0, j, z0, nz, r0, u, lanes) - u * v * v + 0.04


def next_v(ref, j, z0, nz, r0, u, v, lanes):
    return 0.08 * neighbours(ref, 1, j, z0, nz, r0, v, lanes) + (0.42 * v + u * v * v)


def kernel(bricks_in, assign_in, u, v, color_in, alpha_in, u_out, v_out, image, bricks, assign, color, alpha, nodes, a, b, o,
           coded, zbuf, tabs, part, slots, away, came, pair, got, own, pick, stage, lines, tsem, isem, osem, hs, hr, cs, cr,
           ps, pr, fs, fr, lsem):
    t, d = lax.axis_index("tile"), lax.axis_index("dev")
    nt, nd = lax.axis_size("tile"), lax.axis_size("dev")
    tu, td = lax.rem(t + 1, nt), lax.rem(t + nt - 1, nt)
    du, dd = lax.rem(d + 1, nd), lax.rem(d + nd - 1, nd)
    z, y, core = d // 8, lax.rem(d // 2, 4), lax.rem(d, 2)

    def pair_of(yy):
        return 2 * (1 - lax.rem(yy, 2)) + yy // 2

    def chip_of(q):
        return 2 * lax.rem(q, 2) + 1 - q // 2

    fields, outs = (u, v), (u_out, v_out)
    inz = (d > 0, d < nd - 1)
    inx = (t > 0, t < nt - 1)

    def fetch(f, j):
        return pltpu.make_async_copy(
            fields[f].at[:, :, pl.ds(j * 128, 128)], a.at[f, j + 1, pl.ds(2, DZ), pl.ds(ROW0, NR), :], isem.at[f, j])

    smalls = [pltpu.make_async_copy(x, y_, tsem.at[n]) for n, (x, y_) in enumerate(
        ((bricks_in, bricks), (assign_in, assign), (color_in, color), (alpha_in, alpha)))]
    for c in smalls:
        c.start()
    for j in range(LT):
        for f in range(2):
            fetch(f, j).start()

    barrier = pltpu.get_barrier_semaphore()

    def greet(who):
        pl.semaphore_signal(barrier, inc=1, device_id=who, device_id_type=MESH)

    around = [(tt, d2) for tt in (td, t, tu) for d2 in (dd, d, du)]
    around.pop(4)
    for who in around:
        greet(who)

    def chip(k):
        return lax.rem(z + k // 4, 4) * 8 + lax.rem(y + lax.rem(k, 4), 4) * 2 + core

    @pl.loop(1, 16)
    def _(k):
        greet((t, chip(k)))

    shown = lax.rem(d, 4)

    @pl.loop(0, 8)
    def _(k):
        who_t, who_d = lax.rem(t + k // 2, nt), t * 8 + chip_of(shown) * 2 + lax.rem(k, 2)

        @pl.when(jnp.logical_not((who_t == t) & (who_d == d)))
        def _():
            greet((who_t, who_d))

    for c in smalls:
        c.wait()
    for cc in range(4):
        for m in range(4):
            row = color[cc, m : m + 1, :] if cc < 3 else alpha[m : m + 1, :]
            nodes[m, cc : cc + 1, 0:16] = jnp.round(row * (1 / CU if cc < 3 else 1 / AU)).astype(I32)
    lanes = lax.broadcasted_iota(I32, (8, 128), 1)

    @pl.loop(0, LT)
    def _(j):
        rows = []
        for half in range(2):
            m = bricks[d * DZ // 64, t * NR // 64, 2 * j + half]
            rows.append([jnp.broadcast_to(nodes[m, cc][None], (8, 128)) for cc in range(4)])
        for cc in range(4):
            x = jnp.where(lanes < 16, rows[0][cc], pltpu.roll(rows[1][cc], 16, 1))
            tabs[j, cc] = x * 65536 + pltpu.roll(x, 127, 1)

    order = []
    for g in range(4):
        seen = jnp.int32(0)
        found = [jnp.int32(0), jnp.int32(0)]
        for p in range(8):
            w = assign[8 * g + p]
            mine = (w // 8 == t).astype(I32)
            for h in range(2):
                found[h] = found[h] + mine * (seen == h).astype(I32) * lax.rem(w, 8)
            seen = seen + mine
        order += found

    for ref, nz, nr in ((a, DZ + 4, NR + 16), (b, DZ + 2, NR + 8)):
        for f in range(2):
            for j in (0, LT + 1):

                @pl.loop(0, nz)
                def _(k):
                    ref[f, j, k] = jnp.zeros((nr, 128), F32)

    for j in range(LT):
        for f in range(2):
            fetch(f, j).wait()

        @pl.loop(0, 2)
        def _(f):
            for side, z0 in ((0, DZ), (1, 2)):
                for k in range(2):
                    coded[side, j, f, k] = enc(a[f, j + 1, z0 + k, pl.ds(ROW0, NR), :], 1.0)

    pl.semaphore_wait(barrier, 8 + 15 + 8 - ((z == t) & (shown == pair_of(y))).astype(I32))

    copies = []

    def send(src, dst, who):
        n = len(copies)
        c = pltpu.make_async_remote_copy(src_ref=src, dst_ref=dst, send_sem=hs.at[n], recv_sem=hr.at[n], device_id=who, device_id_type=MESH)
        c.start()
        copies.append(c)

    def tile(e, who):
        return jnp.where(who == 1, e, LT - 1 - e)

    wide = LT // CH
    inner, depth = pl.ds(1, LT), pl.ds(2, DZ)
    for k in range(CH):
        js = pl.ds(jnp.minimum(tile(k * wide, 1 - core), tile(k * wide + wide - 1, 1 - core)), wide)
        for side, who in ((0, du), (1, dd)):
            send(coded.at[side, js], zbuf.at[side, js], (t, who))
        if k == 0:
            send(a.at[:, inner, depth, pl.ds(ROW0 + NR - 2, 2), :], a.at[:, inner, depth, pl.ds(ROW0 - 2, 2), :], (tu, d))
            send(a.at[:, inner, depth, pl.ds(ROW0, 2), :], a.at[:, inner, depth, pl.ds(ROW0 + NR, 2), :], (td, d))
        if k == 1:
            for z0, z1, wz in ((DZ + 1, 1, du), (2, DZ + 2, dd)):
                for r0, r1, wx in ((ROW0 + NR - 1, ROW0 - 1, tu), (ROW0, ROW0 + NR, td)):
                    send(a.at[:, inner, z0, pl.ds(r0, 1), :], a.at[:, inner, z1, pl.ds(r1, 1), :], (wx, wz))
    rows_in, corners_in = copies[2:4], copies[6:10]
    layers_in = [copies[0:2], copies[4:6]] + [copies[10 + 2 * k : 12 + 2 * k] for k in range(CH - 2)]

    def first(j, zs, rs):
        def body(r, carry):
            for z0, nz in zs:
                r0 = ROW0 - 1 + 8 * r
                lane = lax.broadcasted_iota(I32, (nz, 8, 128), 2)
                us, vs = cells(a, 0, j, z0, nz, r0), cells(a, 1, j, z0, nz, r0)
                rows = pl.ds(8 * r, 8)
                b[0, j, pl.ds(z0 - 1, nz), rows, :] = next_u(a, j, z0, nz, r0, us, vs, lane)
                b[1, j, pl.ds(z0 - 1, nz), rows, :] = next_v(a, j, z0, nz, r0, us, vs, lane)
            return carry

        lo, hi, step = rs
        lax.fori_loop(0, (hi - lo) // step + 1, lambda i, c: body(lo + step * i, c), 0, unroll=(hi - lo) // step + 1)
        for s in range(2):

            @pl.when(jnp.logical_not(inx[s]))
            def _():
                for f in range(2):
                    for z0, nz in zs:
                        for k in range(z0 - 1, z0 - 1 + nz):
                            b[f, j, k, pl.ds((NR + 1) * s, 1), :] = jnp.zeros((1, 128), F32)

    def second(f, j, zs):
        def body(r, carry):
            for z0, nz in zs:
                r0 = 8 * r + 1
                lane = lax.broadcasted_iota(I32, (nz, 8, 128), 2)
                us, vs = cells(b, 0, j + 1, z0, nz, r0), cells(b, 1, j + 1, z0, nz, r0)
                o[f, j, pl.ds(z0 - 1, nz), pl.ds(8 * r, 8), :] = (next_v if f else next_u)(b, j + 1, z0, nz, r0, us, vs, lane)
            return carry

        lax.fori_loop(0, 8, body, 0, unroll=8)

    offset = jnp.where(lanes >= 64, 16, 0)

    def shade(j, z0, nz, r):
        keep, total = None, [None] * 3
        for k in range(z0, z0 + nz):
            p = jnp.clip(o[1, j, k, pl.ds(8 * r, 8), :] * 15.0, 0.0, 15.0)
            low = p.astype(I32)
            after = p - low.astype(F32)
            idx, here_ = low + offset, 1.0 - after
            vals = []
            for cc in range(4):
                w = gather(tabs[j, cc], idx)
                x = lax.shift_right_logical(w, 16).astype(F32) * here_ + (w & 65535).astype(F32) * after
                vals.append(x.astype(jnp.bfloat16).astype(F32))
            opacity = vals[3] * AU
            w = opacity if keep is None else opacity * keep
            keep = 1.0 - w if keep is None else keep - w
            for cc in range(3):
                x = vals[cc] * w
                total[cc] = x if total[cc] is None else total[cc] + x
        return total, keep

    def emit(f, j):
        return pltpu.make_async_copy(o.at[f, j], outs[f].at[:, :, pl.ds(j * 128, 128)], osem.at[f, j])

    @pl.loop(1, LT + 1)
    def _(j):
        first(j, ((3, 6),), (1, 7, 1))

    for c in rows_in:
        c.wait_recv()
    for s in range(2):

        @pl.when(jnp.logical_not(inx[s]))
        def _():
            @pl.loop(1, LT + 1)
            def _(j):
                for f in range(2):
                    for k in range(2, DZ + 2):
                        a[f, j, k, pl.ds(ROW0 + NR if s else ROW0 - 2, 2), :] = jnp.zeros((2, 128), F32)

    @pl.loop(1, LT + 1)
    def _(j):
        first(j, ((3, 6),), (0, 8, 8))

    @pl.loop(0, LT)
    def _(j):
        second(1, j, ((3, 4),))

    @pl.loop(0, LT)
    def _(j):
        def middle(r, carry):
            total, keep = shade(j, 2, 4, r)
            for cc in range(3):
                part[r, j, cc] = total[cc]
            part[r, j, 3] = keep
            return carry

        lax.fori_loop(0, 8, middle, 0, unroll=8)

    for c in corners_in:
        c.wait_recv()
    for sz in range(2):
        for sx in range(2):

            @pl.when(jnp.logical_not(inz[sz] & inx[sx]))
            def _():
                @pl.loop(1, LT + 1)
                def _(j):
                    for f in range(2):
                        a[f, j, DZ + 2 if sz else 1, pl.ds(ROW0 + NR if sx else ROW0 - 1, 1), :] = jnp.zeros((1, 128), F32)

    def begin(e):
        j = tile(e, core) + 1
        first(j, ((1, 2), (9, 2)), (0, 8, 1))
        for s in range(2):

            @pl.when(jnp.logical_not(inz[s]))
            def _():
                for f in range(2):
                    b[f, j, (DZ + 1) * s] = jnp.zeros((NR + 8, 128), F32)

    def finish(e):
        j = tile(e, core)
        second(1, j, ((1, 2), (7, 2)))
        emit(1, j).start()

        def ends(r, carry):
            front, keep = shade(j, 0, 2, r)
            back, last = shade(j, 6, 2, r)
            mid = part[r, j, 3]
            for cc in range(3):
                part[r, j, cc] = front[cc] + keep * (part[r, j, cc] + mid * back[cc])
            part[r, j, 3] = 1.0 - keep * mid * last
            return carry

        lax.fori_loop(0, 8, ends, 0, unroll=8)

    def put(half):
        for i in range(8):
            for l in range(4):
                for cc in range(4):
                    slots[half, i // 2, cc, pl.ds(2 * l + i % 2, 8, stride=8), :] = part[order[i], 4 * half + l, cc]

    swap = pltpu.make_async_remote_copy(src_ref=away, dst_ref=came, send_sem=cs, recv_sem=cr, device_id=(t, d + 1 - 2 * core), device_id_type=MESH)

    began = done = 0
    for k in range(CH):
        for c in layers_in[k]:
            c.wait_recv()

        @pl.loop(k * wide, (k + 1) * wide)
        def _(e):
            j = tile(e, core)
            for s in range(2):
                for f in range(2):
                    for i in range(2):
                        x = dec(zbuf[s, j, f, i], 1.0)
                        a[f, j + 1, (DZ + 2) * s + i, pl.ds(ROW0, NR), :] = jnp.where(inz[s], x, 0.0)

        ready = (k + 1) * wide
        last = LT if ready == LT else ready - 1
        pl.loop(began, last)(begin)
        began = last
        last = LT if ready == LT else max(began - 1, 0)
        for lo, hi in ((done, min(last, 4)), (max(done, 4), last)):
            if lo < hi:
                pl.loop(lo, hi)(finish)
                if hi == 4:
                    put(1 - core)

                    def pack(i, carry):
                        g, q = i // 4, lax.rem(i, 4)
                        for cc in range(4):
                            away[g, q, cc] = enc(slots[1 - core, g, cc, pl.ds(pl.multiple_of(16 * q, 16), 16), :], TOPS[cc])
                        return carry

                    lax.fori_loop(0, 16, pack, 0, unroll=4)
                    swap.start()
        done = last
    put(core)
    swap.wait_recv()

    def join(i, carry):
        g, q = i // 4, lax.rem(i, 4)
        rows = pl.ds(pl.multiple_of(16 * q, 16), 16)
        x = [slots[core, g, cc, rows, :] for cc in range(4)]
        w = [dec(came[g, q, cc], TOPS[cc]) for cc in range(4)]
        ahead = core == 0
        clear = 1.0 - jnp.where(ahead, x[3], w[3])
        for cc in range(4):
            f, s = jnp.where(ahead, x[cc], w[cc]), jnp.where(ahead, w[cc], x[cc])
            pair[g, q, cc] = enc(f + clear * s, 2 * TOPS[cc])
        return carry

    lax.fori_loop(0, 16, join, 0, unroll=4)

    here = z * 4 + y

    def share(k, dz, dy):
        to_z, to_y = lax.rem(z + dz, 4), lax.rem(y + dy, 4)
        return pltpu.make_async_remote_copy(
            src_ref=pair.at[to_z, pair_of(to_y)], dst_ref=got.at[here], send_sem=ps.at[k], recv_sem=pr.at[k],
            device_id=(t, to_z * 8 + to_y * 2 + core), device_id_type=MESH)

    far = sorted(((dz, dy) for dz in range(4) for dy in range(4) if dz or dy), key=lambda w: -min(w[0], 4 - w[0]) - min(w[1], 4 - w[1]))
    shares = [share(k, dz, dy) for k, (dz, dy) in enumerate(far)]
    for c in shares:
        c.start()
    keep_own = pltpu.make_async_copy(pair.at[z, pair_of(y)], got.at[here], lsem)
    keep_own.start()

    @pl.loop(0, LT)
    def _(j):
        second(0, j, ((1, 8),))
        emit(0, j).start()

    keep_own.wait()
    for c in shares:
        c.wait_recv()

    def fold(s, carry):
        keep, total = carry
        x = [dec(got[s, cc], 2 * TOPS[cc]) for cc in range(4)]
        total = tuple(total[cc] + x[cc] * keep for cc in range(3))
        return keep - keep * x[3], total

    zero = jnp.zeros((16, 128), F32)
    _, total = lax.fori_loop(0, 16, fold, (zero + 1.0, (zero, zero, zero)), unroll=4)
    for cc in range(3):
        own[cc] = total[cc] * CU
        for h in range(2):
            pick[h, cc] = own[cc, pl.ds(h, 8, stride=2), :]

    for p in range(8):
        w = assign[8 * z + p] // 8
        s = jnp.int32(0)
        for q in range(p):
            s = s + (assign[8 * z + q] // 8 == w).astype(I32)
        s = jnp.minimum(s, 1)
        for cc in range(3):
            stage[p, cc] = pick[s, cc]

    def spread(k):
        p = lax.rem(k + d // 4, 8)
        to = 4 * p + pair_of(y)
        return p, (z == t) & (to == d), pltpu.make_async_remote_copy(
            src_ref=stage.at[p], dst_ref=lines.at[t, core], send_sem=fs.at[k], recv_sem=fr.at[t, core],
            device_id=(z, to), device_id_type=MESH)

    @pl.loop(0, 8)
    def _(k):
        p, self_, c = spread(k)

        @pl.when(jnp.logical_not(self_))
        def _():
            c.start()

        @pl.when(self_)
        def _():
            pltpu.make_async_copy(stage.at[p], lines.at[t, core], fr.at[t, core]).start()

    for k in range(8):
        pltpu.make_async_copy(stage.at[0], lines.at[k // 2, k % 2], fr.at[k // 2, k % 2]).wait()

    w = assign[8 * t + d // 4] // 8
    for half in range(2):
        for cc in range(3):
            x = lines[w, half, cc]
            for r in range(2):
                for l in range(4):
                    image[cc, r : r + 1, pl.ds((4 * half + l) * 128, 128)] = x[4 * r + l : 4 * r + l + 1]

    for c in copies + [swap] + shares:
        c.wait_send()

    @pl.loop(0, 8)
    def _(k):
        p, self_, c = spread(k)

        @pl.when(jnp.logical_not(self_))
        def _():
            c.wait_send()

    for j in range(LT):
        for f in range(2):
            emit(f, j).wait()


def local(u, v, bricks, color, alpha, assign):
    hbm = pl.BlockSpec(memory_space=pltpu.HBM)
    vmem = pl.BlockSpec(memory_space=pltpu.VMEM)
    free = pl.BlockSpec(memory_space=pl.ANY)
    dma = pltpu.SemaphoreType.DMA
    return pl.pallas_call(
        kernel,
        out_shape=(
            jax.ShapeDtypeStruct((DZ, NR, NY), F32),
            jax.ShapeDtypeStruct((DZ, NR, NY), F32),
            jax.ShapeDtypeStruct((3, 2, NY), F32),
        ),
        in_specs=[hbm] * 6,
        out_specs=(free, free, vmem),
        scratch_shapes=[
            pltpu.SMEM((4, 4, 16), I32),
            pltpu.SMEM((32,), I32),
            pltpu.VMEM((3, 4, 16), F32),
            pltpu.VMEM((4, 16), F32),
            pltpu.VMEM((4, 4, 128), I32),
            pltpu.VMEM((2, LT + 2, DZ + 4, NR + 16, 128), F32),
            pltpu.VMEM((2, LT + 2, DZ + 2, NR + 8, 128), F32),
            pltpu.VMEM((2, LT, DZ, NR, 128), F32),
            pltpu.VMEM((2, LT, 2, 2, NR, 128), I16),
            pltpu.VMEM((2, LT, 2, 2, NR, 128), I16),
            pltpu.VMEM((LT, 4, 8, 128), I32),
            pltpu.VMEM((NR // 8, LT, 4, 8, 128), F32),
            pltpu.VMEM((2, 4, 4, NR, 128), F32),
            pltpu.VMEM((4, 4, 4, 16, 128), I16),
            pltpu.VMEM((4, 4, 4, 16, 128), I16),
            pltpu.VMEM((4, 4, 4, 16, 128), I16),
            pltpu.VMEM((16, 4, 16, 128), I16),
            pltpu.VMEM((3, 16, 128), F32),
            pltpu.VMEM((2, 3, 8, 128), F32),
            pltpu.VMEM((8, 3, 8, 128), F32),
            pltpu.VMEM((4, 2, 3, 8, 128), F32),
            dma((4,)), dma((2, LT)), dma((2, LT)),
            dma((6 + 2 * CH,)), dma((6 + 2 * CH,)),
            dma, dma,
            dma((16,)), dma((16,)),
            dma((8,)), dma((4, 2)),
            dma,
        ],
        compiler_params=pltpu.CompilerParams(collective_id=0, has_side_effects=True, vmem_limit_bytes=48 << 20),
        name="reaction_render",
    )(bricks, assign, u, v, jnp.transpose(color, (1, 0, 2)), alpha)


def solution(mesh):
    in_specs = (P("dev", "tile", None), P("dev", "tile", None), P(), P(), P(), P())
    out_specs = (P("dev", "tile", None), P("dev", "tile", None), P(None, ("tile", "dev"), None))
    return jax.shard_map(local, mesh=mesh, in_specs=in_specs, out_specs=out_specs, check_vma=False)
```

time: 60.6 us -> 46.6 us (0.77)
  the two profiles are of different devices: /device:TPU:8 before, /device:TPU:1 now
where the time goes in v2:
time: 46.6 us; the launch traced here: 46.4 us
  Pallas kernels  39.8 us (85%)
  local copies, waits for them, and re-layouts  5.96 us (13%)
  between operations  0.65 us (1%)
    pallas_call x1, Pallas kernels, local(): pl.pallas_call(kernel, out_shape=(jax.ShapeDtypeStruct((DZ, NR, NY), F32)...  39.8 us
    unnamed x11, local copies, waits for them, and re-layouts  5.96 us

profile of v2, /device:TPU:1, one launch (start us, length us, event | category | flops | bytes accessed | tf_op | source)
XLA Modules:
  0.0 46.4 jit_solution(3506663760393970405)
XLA Ops:
  0.6 0.0 copy-start
  0.6 0.7 %copy-done = s32[4,4,16]{2,1,0:T(4,128)S(1)} copy-done((s32[4,4,16]{2,1,0:T(4,128)S(1)}, s32[4,4,16]{2,1,0:T(4,128)}, u32[]{:S(2)}) %copy-start) | copy-done | bytes 1048
  1.3 0.0 copy-start.1
  1.3 0.7 %copy-done.1 = f32[4,3,16]{2,0,1:T(4,128)S(1)} copy-done((f32[4,3,16]{2,0,1:T(4,128)S(1)}, f32[4,3,16]{2,0,1:T(4,128)}, u32[]{:S(2)}) %copy-start.1) | copy-done | bytes 792
  2.0 0.0 copy-start.2
  2.0 0.7 %copy-done.2 = f32[4,16]{1,0:T(4,128)S(1)} copy-done((f32[4,16]{1,0:T(4,128)S(1)}, f32[4,16]{1,0:T(4,128)}, u32[]{:S(2)}) %copy-start.2) | copy-done | bytes 280
  2.7 0.0 copy-start.3
  2.7 0.7 %copy-done.3 = s32[32]{0:T(128)S(1)} copy-done((s32[32]{0:T(128)S(1)}, s32[32]{0:T(128)}, u32[]{:S(2)}) %copy-start.3) | copy-done | bytes 152
  3.4 39.8 %reaction_render.1 = (f32[8,64,1024]{2,1,0:T(8,128)S(1)}, f32[8,64,1024]{2,1,0:T(8,128)S(1)}, f32[3,2,1024]{2,1,0:T(2,128)S(1)}) custom-call(s32[4,4,16]{2,1,0:T(4,128)S(1)} %copy-done, s32[32]{0:T(128)S(1)} %copy-done.3, f32[8,64,1024]{2,1,0:T(8,128)} %u.1, f32[8,64,1024]{2,1,0:T(8,128)} %v.1, f32[3,4,16]{2,1,0:T(4,128)S(1)} %bitcast.1, f32[4,16]{1,0:T(4,128)S(1)} %copy-done.2), custom_call_target="tpu_custom_call" | custom-call | tf_op jit(solution)/shard_map/reaction_render/pallas_call | solution.py:475
  43.1 1.3 %copy.12 = f32[8,64,1024]{2,1,0:T(8,128)} copy(f32[8,64,1024]{2,1,0:T(8,128)S(1)} %get-tuple-element.6) | data formatting | bytes 4194304
  44.5 1.3 %copy.13 = f32[8,64,1024]{2,1,0:T(8,128)} copy(f32[8,64,1024]{2,1,0:T(8,128)S(1)} %get-tuple-element.7) | data formatting | bytes 4194304
  45.8 0.6 %copy.14 = f32[3,2,1024]{2,1,0:T(2,128)} copy(f32[3,2,1024]{2,1,0:T(2,128)S(1)} %get-tuple-element.8) | data formatting | bytes 49152
Async XLA Ops:
  0.6 0.7 %copy-start = (s32[4,4,16]{2,1,0:T(4,128)S(1)}, s32[4,4,16]{2,1,0:T(4,128)}, u32[]{:S(2)}) copy-start(s32[4,4,16]{2,1,0:T(4,128)} %bricks_in.1) | copy-start | bytes 3076
  1.3 0.7 %copy-start.1 = (f32[4,3,16]{2,0,1:T(4,128)S(1)}, f32[4,3,16]{2,0,1:T(4,128)}, u32[]{:S(2)}) copy-start(f32[4,3,16]{2,0,1:T(4,128)} %param.9) | copy-start | bytes 2308
  2.0 0.7 %copy-start.2 = (f32[4,16]{1,0:T(4,128)S(1)}, f32[4,16]{1,0:T(4,128)}, u32[]{:S(2)}) copy-start(f32[4,16]{1,0:T(4,128)} %alpha_in.1) | copy-start | bytes 772
  2.7 0.7 %copy-start.3 = (s32[32]{0:T(128)S(1)}, s32[32]{0:T(128)}, u32[]{:S(2)}) copy-start(s32[32]{0:T(128)} %assign_in.1) | copy-start | bytes 388

commit v3 on v2

--- a/solution.py
+++ b/solution.py
@@ -185,6 +185,11 @@
     rows_in, corners_in = copies[2:4], copies[6:10]
     layers_in = [copies[0:2], copies[4:6]] + [copies[10 + 2 * k : 12 + 2 * k] for k in range(CH - 2)]
 
+    def steps(body, rs):
+        lo, hi, step = rs
+        n = (hi - lo) // step + 1
+        lax.fori_loop(0, n, lambda i, c: body(lo + step * i, c), 0, unroll=n)
+
     def first(j, zs, rs):
         def body(r, carry):
             for z0, nz in zs:
@@ -196,8 +201,7 @@
                 b[1, j, pl.ds(z0 - 1, nz), rows, :] = next_v(a, j, z0, nz, r0, us, vs, lane)
             return carry
 
-        lo, hi, step = rs
-        lax.fori_loop(0, (hi - lo) // step + 1, lambda i, c: body(lo + step * i, c), 0, unroll=(hi - lo) // step + 1)
+        steps(body, rs)
         for s in range(2):
 
             @pl.when(jnp.logical_not(inx[s]))
@@ -207,7 +211,7 @@
                         for k in range(z0 - 1, z0 - 1 + nz):
                             b[f, j, k, pl.ds((NR + 1) * s, 1), :] = jnp.zeros((1, 128), F32)
 
-    def second(f, j, zs):
+    def second(f, j, zs, rs=(0, 7, 1)):
         def body(r, carry):
             for z0, nz in zs:
                 r0 = 8 * r + 1
@@ -216,7 +220,7 @@
                 o[f, j, pl.ds(z0 - 1, nz), pl.ds(8 * r, 8), :] = (next_v if f else next_u)(b, j + 1, z0, nz, r0, us, vs, lane)
             return carry
 
-        lax.fori_loop(0, 8, body, 0, unroll=8)
+        steps(body, rs)
 
     offset = jnp.where(lanes >= 64, 16, 0)
 
@@ -243,9 +247,27 @@
     def emit(f, j):
         return pltpu.make_async_copy(o.at[f, j], outs[f].at[:, :, pl.ds(j * 128, 128)], osem.at[f, j])
 
+    def middle(j, rs):
+        def body(r, carry):
+            total, keep = shade(j, 2, 4, r)
+            for cc in range(3):
+                part[r, j, cc] = total[cc]
+            part[r, j, 3] = keep
+            return carry
+
+        steps(body, rs)
+
     @pl.loop(1, LT + 1)
     def _(j):
         first(j, ((3, 6),), (1, 7, 1))
+
+    @pl.loop(0, LT)
+    def _(j):
+        second(1, j, ((3, 4),), (1, 6, 1))
+
+    @pl.loop(0, LT)
+    def _(j):
+        middle(j, (1, 6, 1))
 
     for c in rows_in:
         c.wait_recv()
@@ -259,24 +281,17 @@
                     for k in range(2, DZ + 2):
                         a[f, j, k, pl.ds(ROW0 + NR if s else ROW0 - 2, 2), :] = jnp.zeros((2, 128), F32)
 
-    @pl.loop(1, LT + 1)
+    @pl.loop(1, LT + 1, unroll=2)
     def _(j):
         first(j, ((3, 6),), (0, 8, 8))
 
-    @pl.loop(0, LT)
-    def _(j):
-        second(1, j, ((3, 4),))
-
-    @pl.loop(0, LT)
-    def _(j):
-        def middle(r, carry):
-            total, keep = shade(j, 2, 4, r)
-            for cc in range(3):
-                part[r, j, cc] = total[cc]
-            part[r, j, 3] = keep
-            return carry
-
-        lax.fori_loop(0, 8, middle, 0, unroll=8)
+    @pl.loop(0, LT, unroll=4)
+    def _(j):
+        second(1, j, ((3, 4),), (0, 7, 7))
+
+    @pl.loop(0, LT, unroll=4)
+    def _(j):
+        middle(j, (0, 7, 7))
 
     for c in corners_in:
         c.wait_recv()
@@ -376,6 +391,13 @@
     lax.fori_loop(0, 16, join, 0, unroll=4)
 
     here = z * 4 + y
+    owners = [assign[8 * z + p] // 8 for p in range(8)]
+    which = []
+    for p in range(8):
+        n = jnp.int32(0)
+        for q in range(p):
+            n = n + (owners[q] == owners[p]).astype(I32)
+        which.append(jnp.minimum(n, 1))
 
     def share(k, dz, dy):
         to_z, to_y = lax.rem(z + dz, 4), lax.rem(y + dy, 4)
@@ -413,13 +435,8 @@
             pick[h, cc] = own[cc, pl.ds(h, 8, stride=2), :]
 
     for p in range(8):
-        w = assign[8 * z + p] // 8
-        s = jnp.int32(0)
-        for q in range(p):
-            s = s + (assign[8 * z + q] // 8 == w).astype(I32)
-        s = jnp.minimum(s, 1)
         for cc in range(3):
-            stage[p, cc] = pick[s, cc]
+            stage[p, cc] = pick[which[p], cc]
 
     def spread(k):
         p = lax.rem(k + d // 4, 8)
@@ -467,12 +484,22 @@
             emit(f, j).wait()
 
 
+def write(u, v, image, u_out, v_out, image_out, sem, isem):
+    copies = [pltpu.make_async_copy(image, image_out, isem)]
+    for f, (x, y) in enumerate(((u, u_out), (v, v_out))):
+        copies += [pltpu.make_async_copy(x.at[k], y.at[k], sem.at[f, k]) for k in range(DZ)]
+    for c in copies:
+        c.start()
+    for c in copies:
+        c.wait()
+
+
 def local(u, v, bricks, color, alpha, assign):
     hbm = pl.BlockSpec(memory_space=pltpu.HBM)
     vmem = pl.BlockSpec(memory_space=pltpu.VMEM)
     free = pl.BlockSpec(memory_space=pl.ANY)
     dma = pltpu.SemaphoreType.DMA
-    return pl.pallas_call(
+    u, v, image = pl.pallas_call(
         kernel,
         out_shape=(
             jax.ShapeDtypeStruct((DZ, NR, NY), F32),
@@ -512,7 +539,20 @@
         ],
         compiler_params=pltpu.CompilerParams(collective_id=0, has_side_effects=True, vmem_limit_bytes=48 << 20),
         name="reaction_render",
-    )(bricks, assign, u, v, jnp.transpose(color, (1, 0, 2)), alpha)
+    )(*[pltpu.with_memory_space_constraint(x, pltpu.HBM) for x in (bricks, assign, u, v, jnp.transpose(color, (1, 0, 2)), alpha)])
+    return pl.pallas_call(
+        write,
+        out_shape=(
+            jax.ShapeDtypeStruct((DZ, NR, NY), F32),
+            jax.ShapeDtypeStruct((DZ, NR, NY), F32),
+            jax.ShapeDtypeStruct((3, 2, NY), F32),
+        ),
+        in_specs=[free] * 3,
+        out_specs=(hbm, hbm, hbm),
+        scratch_shapes=[dma((2, DZ)), dma],
+        compiler_params=pltpu.CompilerParams(vmem_limit_bytes=1 << 20),
+        name="write",
+    )(u, v, image)
 
 
 def solution(mesh):

time: 46.6 us -> 40.6 us (0.87)
  local copies, waits for them, and re-layouts: 5.96 us -> 0 us
    unnamed x11 -> x0, local copies, waits for them, and re-layouts: 5.96 us -> none
    pallas_call x0 -> x1, Pallas kernels: none -> 2.15 us  [local(): pl.pallas_call(write, out_shape=(jax.ShapeDtypeStruct((DZ, NR, NY), F32),...]
    pallas_call x1, Pallas kernels: 39.8 us -> 37.7 us  [local(): pl.pallas_call(kernel, out_shape=(jax.ShapeDtypeStruct((DZ, NR, NY), F32)...]
where the time goes in v3:
time: 40.6 us; the launch traced here: 40.5 us
  Pallas kernels  39.9 us (98%)
  between operations  0.64 us (2%)
    pallas_call x1, Pallas kernels, local(): pl.pallas_call(kernel, out_shape=(jax.ShapeDtypeStruct((DZ, NR, NY), F32)...  37.7 us
    pallas_call x1, Pallas kernels, local(): pl.pallas_call(write, out_shape=(jax.ShapeDtypeStruct((DZ, NR, NY), F32),...  2.15 us

profile of v3, /device:TPU:1, one launch (start us, length us, event | category | flops | bytes accessed | tf_op | source)
XLA Modules:
  0.0 40.5 jit_solution(16154216977857704776)
XLA Ops:
  0.6 37.7 %reaction_render.1 = (f32[8,64,1024]{2,1,0:T(8,128)S(1)}, f32[8,64,1024]{2,1,0:T(8,128)S(1)}, f32[3,2,1024]{2,1,0:T(2,128)S(1)}) custom-call(s32[4,4,16]{2,1,0:T(4,128)} %bricks_in.1, s32[32]{0:T(128)} %assign_in.1, f32[8,64,1024]{2,1,0:T(8,128)} %u.1, f32[8,64,1024]{2,1,0:T(8,128)} %v.1, f32[3,4,16]{2,1,0:T(4,128)} %bitcast.1, f32[4,16]{1,0:T(4,128)} %alpha_in.1), custom_call_target="tpu_custom_call" | custom-call | tf_op jit(solution)/shard_map/reaction_render/pallas_call | solution.py:502
  38.4 2.2 %write.1 = (f32[8,64,1024]{2,1,0:T(8,128)}, f32[8,64,1024]{2,1,0:T(8,128)}, f32[3,2,1024]{2,1,0:T(2,128)}) custom-call(f32[8,64,1024]{2,1,0:T(8,128)S(1)} %get-tuple-element.6.u, f32[8,64,1024]{2,1,0:T(8,128)S(1)} %get-tuple-element.7.v, f32[3,2,1024]{2,1,0:T(2,128)S(1)} %get-tuple-element.8.image), custom_call_target="tpu_custom_call" | custom-call | tf_op jit(solution)/shard_map/write/pallas_call | solution.py:543

commit v4 on v3

--- a/solution.py
+++ b/solution.py
@@ -15,6 +15,7 @@
 CU, AU = 2.0**-14, 2.0**-21
 STEPS, SHIFT = 65534.0, 32767.0
 TOPS = (0.32 / CU, 0.32 / CU, 0.32 / CU, 0.16)
+TOP = 2.01 / CU
 CH = 4
 
 
@@ -50,8 +51,8 @@
     return 0.08 * neighbours(ref, 1, j, z0, nz, r0, v, lanes) + (0.42 * v + u * v * v)
 
 
-def kernel(bricks_in, assign_in, u, v, color_in, alpha_in, u_out, v_out, image, bricks, assign, color, alpha, nodes, a, b, o,
-           coded, zbuf, tabs, part, slots, away, came, pair, got, own, pick, stage, lines, tsem, isem, osem, hs, hr, cs, cr,
+def kernel(bricks_in, assign_in, u, v, color_in, alpha_in, u_out, v_out, image, bricks, assign, color, alpha, nodes, unit, a, b, o,
+           coded, zbuf, tabs, part, slots, away, came, pair, got, own, pick, stage, lines, told, tsem, isem, osem, hs, hr, cs, cr,
            ps, pr, fs, fr, lsem):
     t, d = lax.axis_index("tile"), lax.axis_index("dev")
     nt, nd = lax.axis_size("tile"), lax.axis_size("dev")
@@ -77,9 +78,12 @@
         ((bricks_in, bricks), (assign_in, assign), (color_in, color), (alpha_in, alpha)))]
     for c in smalls:
         c.start()
-    for j in range(LT):
+    def tile(e, who):
+        return jnp.where(who == 1, e, LT - 1 - e)
+
+    for e in range(LT):
         for f in range(2):
-            fetch(f, j).start()
+            fetch(f, tile(e, 1 - core)).start()
 
     barrier = pltpu.get_barrier_semaphore()
 
@@ -88,32 +92,43 @@
 
     around = [(tt, d2) for tt in (td, t, tu) for d2 in (dd, d, du)]
     around.pop(4)
+    def chip(zz, yy):
+        return (t, lax.rem(zz, 4) * 8 + lax.rem(yy, 4) * 2 + core)
+
+    sides_y = (chip(z, y + 1), chip(z, y + 3))
+    sides_z = (chip(z + 1, y), chip(z + 3, y))
+    sides_x = ((tu, d), (td, d))
+    around += sides_y + sides_z
     for who in around:
         greet(who)
 
-    def chip(k):
-        return lax.rem(z + k // 4, 4) * 8 + lax.rem(y + lax.rem(k, 4), 4) * 2 + core
-
-    @pl.loop(1, 16)
-    def _(k):
-        greet((t, chip(k)))
-
     shown = lax.rem(d, 4)
 
-    @pl.loop(0, 8)
-    def _(k):
-        who_t, who_d = lax.rem(t + k // 2, nt), t * 8 + chip_of(shown) * 2 + lax.rem(k, 2)
-
-        @pl.when(jnp.logical_not((who_t == t) & (who_d == d)))
-        def _():
-            greet((who_t, who_d))
+    rounds = (sides_y, sides_z, sides_z, sides_x, sides_x, ((t, d + 1 - 2 * core),))
+
+    def tell(n):
+        for who in rounds[n]:
+            pl.semaphore_signal(told.at[n], inc=1, device_id=who, device_id_type=MESH)
+
+    def hear(n):
+        pl.semaphore_wait(told.at[n], len(rounds[n]))
+        if n + 1 < len(rounds):
+            tell(n + 1)
 
     for c in smalls:
         c.wait()
+    largest = color[0]
+    for cc in (1, 2):
+        largest = jnp.maximum(largest, color[cc])
+    largest = jnp.max(jnp.max(largest, axis=0, keepdims=True), axis=1, keepdims=True)
+    up = jnp.ones((1, 1), F32)
+    for n in (8, 4, 2, 1):
+        up = jnp.where(largest * up * 2.0**n <= 2.0, up * 2.0**n, up)
+    unit[...] = jnp.broadcast_to(up, (8, 128))
     for cc in range(4):
         for m in range(4):
             row = color[cc, m : m + 1, :] if cc < 3 else alpha[m : m + 1, :]
-            nodes[m, cc : cc + 1, 0:16] = jnp.round(row * (1 / CU if cc < 3 else 1 / AU)).astype(I32)
+            nodes[m, cc : cc + 1, 0:16] = jnp.round(row * up * (1 / CU) if cc < 3 else row * (1 / AU)).astype(I32)
     lanes = lax.broadcasted_iota(I32, (8, 128), 1)
 
     @pl.loop(0, LT)
@@ -146,18 +161,6 @@
                 def _(k):
                     ref[f, j, k] = jnp.zeros((nr, 128), F32)
 
-    for j in range(LT):
-        for f in range(2):
-            fetch(f, j).wait()
-
-        @pl.loop(0, 2)
-        def _(f):
-            for side, z0 in ((0, DZ), (1, 2)):
-                for k in range(2):
-                    coded[side, j, f, k] = enc(a[f, j + 1, z0 + k, pl.ds(ROW0, NR), :], 1.0)
-
-    pl.semaphore_wait(barrier, 8 + 15 + 8 - ((z == t) & (shown == pair_of(y))).astype(I32))
-
     copies = []
 
     def send(src, dst, who):
@@ -166,32 +169,42 @@
         c.start()
         copies.append(c)
 
-    def tile(e, who):
-        return jnp.where(who == 1, e, LT - 1 - e)
-
     wide = LT // CH
     inner, depth = pl.ds(1, LT), pl.ds(2, DZ)
     for k in range(CH):
+
+        @pl.loop(k * wide, (k + 1) * wide)
+        def _(e):
+            j = tile(e, 1 - core)
+            for f in range(2):
+                fetch(f, j).wait()
+                for side, z0 in ((0, DZ), (1, 2)):
+                    for i in range(2):
+                        coded[side, j, f, i] = enc(a[f, j + 1, z0 + i, pl.ds(ROW0, NR), :], 1.0)
+
+        if k == 0:
+            pl.semaphore_wait(barrier, len(around))
+            tell(0)
         js = pl.ds(jnp.minimum(tile(k * wide, 1 - core), tile(k * wide + wide - 1, 1 - core)), wide)
         for side, who in ((0, du), (1, dd)):
             send(coded.at[side, js], zbuf.at[side, js], (t, who))
-        if k == 0:
+        if k == CH - 1:
             send(a.at[:, inner, depth, pl.ds(ROW0 + NR - 2, 2), :], a.at[:, inner, depth, pl.ds(ROW0 - 2, 2), :], (tu, d))
             send(a.at[:, inner, depth, pl.ds(ROW0, 2), :], a.at[:, inner, depth, pl.ds(ROW0 + NR, 2), :], (td, d))
-        if k == 1:
+        if k == CH - 1:
             for z0, z1, wz in ((DZ + 1, 1, du), (2, DZ + 2, dd)):
                 for r0, r1, wx in ((ROW0 + NR - 1, ROW0 - 1, tu), (ROW0, ROW0 + NR, td)):
                     send(a.at[:, inner, z0, pl.ds(r0, 1), :], a.at[:, inner, z1, pl.ds(r1, 1), :], (wx, wz))
-    rows_in, corners_in = copies[2:4], copies[6:10]
-    layers_in = [copies[0:2], copies[4:6]] + [copies[10 + 2 * k : 12 + 2 * k] for k in range(CH - 2)]
+    layers_in = [copies[2 * k : 2 * k + 2] for k in range(CH)]
+    rows_in, corners_in = copies[2 * CH : 2 * CH + 2], copies[2 * CH + 2 :]
 
     def steps(body, rs):
         lo, hi, step = rs
         n = (hi - lo) // step + 1
         lax.fori_loop(0, n, lambda i, c: body(lo + step * i, c), 0, unroll=n)
 
-    def first(j, zs, rs):
-        def body(r, carry):
+    def first(j, zs, rs, outer=()):
+        def body(r, carry, zs=zs):
             for z0, nz in zs:
                 r0 = ROW0 - 1 + 8 * r
                 lane = lax.broadcasted_iota(I32, (nz, 8, 128), 2)
@@ -202,17 +215,19 @@
             return carry
 
         steps(body, rs)
+        if outer:
+            steps(lambda r, c: body(r, c, outer), (0, 8, 8))
         for s in range(2):
 
             @pl.when(jnp.logical_not(inx[s]))
             def _():
                 for f in range(2):
-                    for z0, nz in zs:
+                    for z0, nz in zs + outer:
                         for k in range(z0 - 1, z0 - 1 + nz):
                             b[f, j, k, pl.ds((NR + 1) * s, 1), :] = jnp.zeros((1, 128), F32)
 
-    def second(f, j, zs, rs=(0, 7, 1)):
-        def body(r, carry):
+    def second(f, j, zs, rs=(0, 7, 1), outer=()):
+        def body(r, carry, zs=zs):
             for z0, nz in zs:
                 r0 = 8 * r + 1
                 lane = lax.broadcasted_iota(I32, (nz, 8, 128), 2)
@@ -221,6 +236,8 @@
             return carry
 
         steps(body, rs)
+        if outer:
+            steps(lambda r, c: body(r, c, outer), (0, 7, 7))
 
     offset = jnp.where(lanes >= 64, 16, 0)
 
@@ -261,14 +278,19 @@
     def _(j):
         first(j, ((3, 6),), (1, 7, 1))
 
+
     @pl.loop(0, LT)
     def _(j):
         second(1, j, ((3, 4),), (1, 6, 1))
 
-    @pl.loop(0, LT)
+
+    hear(0)
+
+    @pl.loop(0, LT, unroll=2)
     def _(j):
         middle(j, (1, 6, 1))
 
+    hear(1)
     for c in rows_in:
         c.wait_recv()
     for s in range(2):
@@ -281,18 +303,6 @@
                     for k in range(2, DZ + 2):
                         a[f, j, k, pl.ds(ROW0 + NR if s else ROW0 - 2, 2), :] = jnp.zeros((2, 128), F32)
 
-    @pl.loop(1, LT + 1, unroll=2)
-    def _(j):
-        first(j, ((3, 6),), (0, 8, 8))
-
-    @pl.loop(0, LT, unroll=4)
-    def _(j):
-        second(1, j, ((3, 4),), (0, 7, 7))
-
-    @pl.loop(0, LT, unroll=4)
-    def _(j):
-        middle(j, (0, 7, 7))
-
     for c in corners_in:
         c.wait_recv()
     for sz in range(2):
@@ -307,7 +317,7 @@
 
     def begin(e):
         j = tile(e, core) + 1
-        first(j, ((1, 2), (9, 2)), (0, 8, 1))
+        first(j, ((1, 2), (9, 2)), (0, 8, 1), ((3, 6),))
         for s in range(2):
 
             @pl.when(jnp.logical_not(inz[s]))
@@ -317,7 +327,7 @@
 
     def finish(e):
         j = tile(e, core)
-        second(1, j, ((1, 2), (7, 2)))
+        second(1, j, ((1, 2), (7, 2)), outer=((3, 4),))
         emit(1, j).start()
 
         def ends(r, carry):
@@ -329,7 +339,15 @@
             part[r, j, 3] = 1.0 - keep * mid * last
             return carry
 
-        lax.fori_loop(0, 8, ends, 0, unroll=8)
+        def whole(r, carry):
+            total, keep = shade(j, 0, DZ, r)
+            for cc in range(3):
+                part[r, j, cc] = total[cc]
+            part[r, j, 3] = 1.0 - keep
+            return carry
+
+        steps(ends, (1, 6, 1))
+        steps(whole, (0, 7, 7))
 
     def put(half):
         for i in range(8):
@@ -371,6 +389,7 @@
                         return carry
 
                     lax.fori_loop(0, 16, pack, 0, unroll=4)
+                    hear(2)
                     swap.start()
         done = last
     put(core)
@@ -412,12 +431,14 @@
     keep_own = pltpu.make_async_copy(pair.at[z, pair_of(y)], got.at[here], lsem)
     keep_own.start()
 
+    hear(3)
     @pl.loop(0, LT)
     def _(j):
         second(0, j, ((1, 8),))
         emit(0, j).start()
 
     keep_own.wait()
+    hear(4)
     for c in shares:
         c.wait_recv()
 
@@ -430,13 +451,16 @@
     zero = jnp.zeros((16, 128), F32)
     _, total = lax.fori_loop(0, 16, fold, (zero + 1.0, (zero, zero, zero)), unroll=4)
     for cc in range(3):
-        own[cc] = total[cc] * CU
+        own[cc] = total[cc]
         for h in range(2):
             pick[h, cc] = own[cc, pl.ds(h, 8, stride=2), :]
 
     for p in range(8):
-        for cc in range(3):
-            stage[p, cc] = pick[which[p], cc]
+        red, green, blue = (pick[which[p], cc] for cc in range(3))
+        stage[p, 0] = enc(jnp.concatenate([red, green], axis=0), TOP)
+        stage[p, 1] = enc(jnp.concatenate([blue, blue], axis=0), TOP)
+
+    hear(5)
 
     def spread(k):
         p = lax.rem(k + d // 4, 8)
@@ -461,12 +485,14 @@
         pltpu.make_async_copy(stage.at[0], lines.at[k // 2, k % 2], fr.at[k // 2, k % 2]).wait()
 
     w = assign[8 * t + d // 4] // 8
+    scale = CU / unit[...]
     for half in range(2):
+        x = [dec(lines[w, half, n], TOP) for n in range(2)]
         for cc in range(3):
-            x = lines[w, half, cc]
+            x_ = x[cc // 2][8 * (cc % 2) : 8 * (cc % 2) + 8] * scale
             for r in range(2):
                 for l in range(4):
-                    image[cc, r : r + 1, pl.ds((4 * half + l) * 128, 128)] = x[4 * r + l : 4 * r + l + 1]
+                    image[cc, r : r + 1, pl.ds((4 * half + l) * 128, 128)] = x_[4 * r + l : 4 * r + l + 1]
 
     for c in copies + [swap] + shares:
         c.wait_send()
@@ -514,6 +540,7 @@
             pltpu.VMEM((3, 4, 16), F32),
             pltpu.VMEM((4, 16), F32),
             pltpu.VMEM((4, 4, 128), I32),
+            pltpu.VMEM((8, 128), F32),
             pltpu.VMEM((2, LT + 2, DZ + 4, NR + 16, 128), F32),
             pltpu.VMEM((2, LT + 2, DZ + 2, NR + 8, 128), F32),
             pltpu.VMEM((2, LT, DZ, NR, 128), F32),
@@ -528,8 +555,9 @@
             pltpu.VMEM((16, 4, 16, 128), I16),
             pltpu.VMEM((3, 16, 128), F32),
             pltpu.VMEM((2, 3, 8, 128), F32),
-            pltpu.VMEM((8, 3, 8, 128), F32),
-            pltpu.VMEM((4, 2, 3, 8, 128), F32),
+            pltpu.VMEM((8, 2, 16, 128), I16),
+            pltpu.VMEM((4, 2, 2, 16, 128), I16),
+            pltpu.SemaphoreType.REGULAR((6,)),
             dma((4,)), dma((2, LT)), dma((2, LT)),
             dma((6 + 2 * CH,)), dma((6 + 2 * CH,)),
             dma, dma,

time: 40.6 us -> 38.8 us (0.956)
  Pallas kernels: 39.9 us -> 38 us
    pallas_call x1, Pallas kernels: 37.7 us -> 35.9 us  [local(): pl.pallas_call(kernel, out_shape=(jax.ShapeDtypeStruct((DZ, NR, NY), F32)...]
where the time goes in v4:
time: 38.8 us; the launch traced here: 38.7 us
  Pallas kernels  38 us (98%)
  between operations  0.64 us (2%)
    pallas_call x1, Pallas kernels, local(): pl.pallas_call(kernel, out_shape=(jax.ShapeDtypeStruct((DZ, NR, NY), F32)...  35.9 us
    pallas_call x1, Pallas kernels, local(): pl.pallas_call(write, out_shape=(jax.ShapeDtypeStruct((DZ, NR, NY), F32),...  2.15 us

profile of v4, /device:TPU:1, one launch (start us, length us, event | category | flops | bytes accessed | tf_op | source)
XLA Modules:
  0.0 38.7 jit_solution(1395517083335709956)
XLA Ops:
  0.6 35.9 %reaction_render.1 = (f32[8,64,1024]{2,1,0:T(8,128)S(1)}, f32[8,64,1024]{2,1,0:T(8,128)S(1)}, f32[3,2,1024]{2,1,0:T(2,128)S(1)}) custom-call(s32[4,4,16]{2,1,0:T(4,128)} %bricks_in.1, s32[32]{0:T(128)} %assign_in.1, f32[8,64,1024]{2,1,0:T(8,128)} %u.1, f32[8,64,1024]{2,1,0:T(8,128)} %v.1, f32[3,4,16]{2,1,0:T(4,128)} %bitcast.1, f32[4,16]{1,0:T(4,128)} %alpha_in.1), custom_call_target="tpu_custom_call" | custom-call | tf_op jit(solution)/shard_map/reaction_render/pallas_call | solution.py:528
  36.5 2.2 %write.1 = (f32[8,64,1024]{2,1,0:T(8,128)}, f32[8,64,1024]{2,1,0:T(8,128)}, f32[3,2,1024]{2,1,0:T(2,128)}) custom-call(f32[8,64,1024]{2,1,0:T(8,128)S(1)} %get-tuple-element.6.u, f32[8,64,1024]{2,1,0:T(8,128)S(1)} %get-tuple-element.7.v, f32[3,2,1024]{2,1,0:T(2,128)S(1)} %get-tuple-element.8.image), custom_call_target="tpu_custom_call" | custom-call | tf_op jit(solution)/shard_map/write/pallas_call | solution.py:571

commit v5 on v4

--- a/solution.py
+++ b/solution.py
@@ -59,6 +59,11 @@
     tu, td = lax.rem(t + 1, nt), lax.rem(t + nt - 1, nt)
     du, dd = lax.rem(d + 1, nd), lax.rem(d + nd - 1, nd)
     z, y, core = d // 8, lax.rem(d // 2, 4), lax.rem(d, 2)
+
+    def group_of(zz):
+        return lax.rem(zz + nt - t, nt)
+
+    group = group_of(z)
 
     def pair_of(yy):
         return 2 * (1 - lax.rem(yy, 2)) + yy // 2
@@ -161,8 +166,6 @@
                 def _(k):
                     ref[f, j, k] = jnp.zeros((nr, 128), F32)
 
-    copies = []
-
     def send(src, dst, who):
         n = len(copies)
         c = pltpu.make_async_remote_copy(src_ref=src, dst_ref=dst, send_sem=hs.at[n], recv_sem=hr.at[n], device_id=who, device_id_type=MESH)
@@ -171,8 +174,15 @@
 
     wide = LT // CH
     inner, depth = pl.ds(1, LT), pl.ds(2, DZ)
-    for k in range(CH):
-
+    def layers(k, side):
+        js = pl.ds(jnp.minimum(tile(k * wide, 1 - core), tile(k * wide + wide - 1, 1 - core)), wide)
+        n = 2 * k + side
+        return pltpu.make_async_remote_copy(
+            src_ref=coded.at[side, js], dst_ref=zbuf.at[side, js], send_sem=hs.at[n], recv_sem=hr.at[n],
+            device_id=(t, (du, dd)[side]), device_id_type=MESH)
+
+    @pl.loop(0, CH)
+    def _(k):
         @pl.loop(k * wide, (k + 1) * wide)
         def _(e):
             j = tile(e, 1 - core)
@@ -182,20 +192,20 @@
                     for i in range(2):
                         coded[side, j, f, i] = enc(a[f, j + 1, z0 + i, pl.ds(ROW0, NR), :], 1.0)
 
-        if k == 0:
+        @pl.when(k == 0)
+        def _():
             pl.semaphore_wait(barrier, len(around))
             tell(0)
-        js = pl.ds(jnp.minimum(tile(k * wide, 1 - core), tile(k * wide + wide - 1, 1 - core)), wide)
-        for side, who in ((0, du), (1, dd)):
-            send(coded.at[side, js], zbuf.at[side, js], (t, who))
-        if k == CH - 1:
-            send(a.at[:, inner, depth, pl.ds(ROW0 + NR - 2, 2), :], a.at[:, inner, depth, pl.ds(ROW0 - 2, 2), :], (tu, d))
-            send(a.at[:, inner, depth, pl.ds(ROW0, 2), :], a.at[:, inner, depth, pl.ds(ROW0 + NR, 2), :], (td, d))
-        if k == CH - 1:
-            for z0, z1, wz in ((DZ + 1, 1, du), (2, DZ + 2, dd)):
-                for r0, r1, wx in ((ROW0 + NR - 1, ROW0 - 1, tu), (ROW0, ROW0 + NR, td)):
-                    send(a.at[:, inner, z0, pl.ds(r0, 1), :], a.at[:, inner, z1, pl.ds(r1, 1), :], (wx, wz))
-    layers_in = [copies[2 * k : 2 * k + 2] for k in range(CH)]
+
+        for side in range(2):
+            layers(k, side).start()
+
+    copies = [layers(k, side) for k in range(CH) for side in range(2)]
+    send(a.at[:, inner, depth, pl.ds(ROW0 + NR - 2, 2), :], a.at[:, inner, depth, pl.ds(ROW0 - 2, 2), :], (tu, d))
+    send(a.at[:, inner, depth, pl.ds(ROW0, 2), :], a.at[:, inner, depth, pl.ds(ROW0 + NR, 2), :], (td, d))
+    for z0, z1, wz in ((DZ + 1, 1, du), (2, DZ + 2, dd)):
+        for r0, r1, wx in ((ROW0 + NR - 1, ROW0 - 1, tu), (ROW0, ROW0 + NR, td)):
+            send(a.at[:, inner, z0, pl.ds(r0, 1), :], a.at[:, inner, z1, pl.ds(r1, 1), :], (wx, wz))
     rows_in, corners_in = copies[2 * CH : 2 * CH + 2], copies[2 * CH + 2 :]
 
     def steps(body, rs):
@@ -205,13 +215,12 @@
 
     def first(j, zs, rs, outer=()):
         def body(r, carry, zs=zs):
-            for z0, nz in zs:
+            for z0, nz, fs in zs:
                 r0 = ROW0 - 1 + 8 * r
                 lane = lax.broadcasted_iota(I32, (nz, 8, 128), 2)
                 us, vs = cells(a, 0, j, z0, nz, r0), cells(a, 1, j, z0, nz, r0)
-                rows = pl.ds(8 * r, 8)
-                b[0, j, pl.ds(z0 - 1, nz), rows, :] = next_u(a, j, z0, nz, r0, us, vs, lane)
-                b[1, j, pl.ds(z0 - 1, nz), rows, :] = next_v(a, j, z0, nz, r0, us, vs, lane)
+                for f in fs:
+                    b[f, j, pl.ds(z0 - 1, nz), pl.ds(8 * r, 8), :] = (next_v if f else next_u)(a, j, z0, nz, r0, us, vs, lane)
             return carry
 
         steps(body, rs)
@@ -221,9 +230,9 @@
 
             @pl.when(jnp.logical_not(inx[s]))
             def _():
-                for f in range(2):
-                    for z0, nz in zs + outer:
-                        for k in range(z0 - 1, z0 - 1 + nz):
+                for z0, nz, fs in zs + outer:
+                    for k in range(z0 - 1, z0 - 1 + nz):
+                        for f in fs:
                             b[f, j, k, pl.ds((NR + 1) * s, 1), :] = jnp.zeros((1, 128), F32)
 
     def second(f, j, zs, rs=(0, 7, 1), outer=()):
@@ -276,10 +285,10 @@
 
     @pl.loop(1, LT + 1)
     def _(j):
-        first(j, ((3, 6),), (1, 7, 1))
-
-
-    @pl.loop(0, LT)
+        first(j, ((3, 6, (0, 1)),), (1, 7, 1))
+
+
+    @pl.loop(0, LT, unroll=2)
     def _(j):
         second(1, j, ((3, 4),), (1, 6, 1))
 
@@ -317,37 +326,39 @@
 
     def begin(e):
         j = tile(e, core) + 1
-        first(j, ((1, 2), (9, 2)), (0, 8, 1), ((3, 6),))
+        first(j, ((2, 1, (0,)), (9, 1, (0,)), (1, 2, (1,)), (9, 2, (1,))), (0, 8, 1), ((3, 6, (0, 1)),))
         for s in range(2):
 
             @pl.when(jnp.logical_not(inz[s]))
             def _():
-                for f in range(2):
-                    b[f, j, (DZ + 1) * s] = jnp.zeros((NR + 8, 128), F32)
-
-    def finish(e):
-        j = tile(e, core)
-        second(1, j, ((1, 2), (7, 2)), outer=((3, 4),))
-        emit(1, j).start()
-
-        def ends(r, carry):
-            front, keep = shade(j, 0, 2, r)
-            back, last = shade(j, 6, 2, r)
-            mid = part[r, j, 3]
-            for cc in range(3):
-                part[r, j, cc] = front[cc] + keep * (part[r, j, cc] + mid * back[cc])
-            part[r, j, 3] = 1.0 - keep * mid * last
-            return carry
-
-        def whole(r, carry):
-            total, keep = shade(j, 0, DZ, r)
-            for cc in range(3):
-                part[r, j, cc] = total[cc]
-            part[r, j, 3] = 1.0 - keep
-            return carry
-
-        steps(ends, (1, 6, 1))
-        steps(whole, (0, 7, 7))
+                b[1, j, (DZ + 1) * s] = jnp.zeros((NR + 8, 128), F32)
+
+    def finish(i):
+        js = [tile(2 * i + n, core) for n in range(2)]
+        for j in js:
+            second(1, j, ((1, 2), (7, 2)), outer=((3, 4),))
+        for j in js:
+
+            def ends(r, carry):
+                front, keep = shade(j, 0, 2, r)
+                back, last = shade(j, 6, 2, r)
+                mid = part[r, j, 3]
+                for cc in range(3):
+                    part[r, j, cc] = front[cc] + keep * (part[r, j, cc] + mid * back[cc])
+                part[r, j, 3] = 1.0 - keep * mid * last
+                return carry
+
+            def whole(r, carry):
+                total, keep = shade(j, 0, DZ, r)
+                for cc in range(3):
+                    part[r, j, cc] = total[cc]
+                part[r, j, 3] = 1.0 - keep
+                return carry
+
+            steps(ends, (1, 6, 1))
+            steps(whole, (0, 7, 7))
+        for j in js:
+            emit(1, j).start()
 
     def put(half):
         for i in range(8):
@@ -357,10 +368,10 @@
 
     swap = pltpu.make_async_remote_copy(src_ref=away, dst_ref=came, send_sem=cs, recv_sem=cr, device_id=(t, d + 1 - 2 * core), device_id_type=MESH)
 
-    began = done = 0
-    for k in range(CH):
-        for c in layers_in[k]:
-            c.wait_recv()
+    @pl.loop(0, CH)
+    def _(k):
+        for side in range(2):
+            layers(k, side).wait_recv()
 
         @pl.loop(k * wide, (k + 1) * wide)
         def _(e):
@@ -371,27 +382,24 @@
                         x = dec(zbuf[s, j, f, i], 1.0)
                         a[f, j + 1, (DZ + 2) * s + i, pl.ds(ROW0, NR), :] = jnp.where(inz[s], x, 0.0)
 
-        ready = (k + 1) * wide
-        last = LT if ready == LT else ready - 1
-        pl.loop(began, last)(begin)
-        began = last
-        last = LT if ready == LT else max(began - 1, 0)
-        for lo, hi in ((done, min(last, 4)), (max(done, 4), last)):
-            if lo < hi:
-                pl.loop(lo, hi)(finish)
-                if hi == 4:
-                    put(1 - core)
-
-                    def pack(i, carry):
-                        g, q = i // 4, lax.rem(i, 4)
-                        for cc in range(4):
-                            away[g, q, cc] = enc(slots[1 - core, g, cc, pl.ds(pl.multiple_of(16 * q, 16), 16), :], TOPS[cc])
-                        return carry
-
-                    lax.fori_loop(0, 16, pack, 0, unroll=4)
-                    hear(2)
-                    swap.start()
-        done = last
+        end = k == CH - 1
+        pl.loop(jnp.maximum(wide * k - 1, 0), jnp.where(end, LT, wide * k + 1))(begin)
+        pl.loop(jnp.maximum(k - 1, 0), jnp.where(end, LT // 2, k))(finish)
+
+        @pl.when(k == CH // 2)
+        def _():
+            put(1 - core)
+
+            def pack(i, carry):
+                g, q = i // 4, lax.rem(i, 4)
+                for cc in range(4):
+                    away[g, q, cc] = enc(slots[1 - core, g, cc, pl.ds(pl.multiple_of(16 * q, 16), 16), :], TOPS[cc])
+                return carry
+
+            lax.fori_loop(0, 16, pack, 0, unroll=4)
+            hear(2)
+            swap.start()
+
     put(core)
     swap.wait_recv()
 
@@ -410,7 +418,7 @@
     lax.fori_loop(0, 16, join, 0, unroll=4)
 
     here = z * 4 + y
-    owners = [assign[8 * z + p] // 8 for p in range(8)]
+    owners = [assign[8 * group + p] // 8 for p in range(8)]
     which = []
     for p in range(8):
         n = jnp.int32(0)
@@ -421,17 +429,26 @@
     def share(k, dz, dy):
         to_z, to_y = lax.rem(z + dz, 4), lax.rem(y + dy, 4)
         return pltpu.make_async_remote_copy(
-            src_ref=pair.at[to_z, pair_of(to_y)], dst_ref=got.at[here], send_sem=ps.at[k], recv_sem=pr.at[k],
+            src_ref=pair.at[group_of(to_z), pair_of(to_y)], dst_ref=got.at[here], send_sem=ps.at[k], recv_sem=pr.at[k],
             device_id=(t, to_z * 8 + to_y * 2 + core), device_id_type=MESH)
 
     far = sorted(((dz, dy) for dz in range(4) for dy in range(4) if dz or dy), key=lambda w: -min(w[0], 4 - w[0]) - min(w[1], 4 - w[1]))
     shares = [share(k, dz, dy) for k, (dz, dy) in enumerate(far)]
     for c in shares:
         c.start()
-    keep_own = pltpu.make_async_copy(pair.at[z, pair_of(y)], got.at[here], lsem)
+    keep_own = pltpu.make_async_copy(pair.at[group, pair_of(y)], got.at[here], lsem)
     keep_own.start()
 
     hear(3)
+    @pl.loop(1, LT + 1)
+    def _(j):
+        first(j, ((1, 1, (0,)), (DZ + 2, 1, (0,))), (0, 8, 1))
+        for s in range(2):
+
+            @pl.when(jnp.logical_not(inz[s]))
+            def _():
+                b[0, j, (DZ + 1) * s] = jnp.zeros((NR + 8, 128), F32)
+
     @pl.loop(0, LT)
     def _(j):
         second(0, j, ((1, 8),))
@@ -465,9 +482,9 @@
     def spread(k):
         p = lax.rem(k + d // 4, 8)
         to = 4 * p + pair_of(y)
-        return p, (z == t) & (to == d), pltpu.make_async_remote_copy(
+        return p, (group == t) & (to == d), pltpu.make_async_remote_copy(
             src_ref=stage.at[p], dst_ref=lines.at[t, core], send_sem=fs.at[k], recv_sem=fr.at[t, core],
-            device_id=(z, to), device_id_type=MESH)
+            device_id=(group, to), device_id_type=MESH)
 
     @pl.loop(0, 8)
     def _(k):

time: 38.8 us -> 37.8 us (0.974)
  Pallas kernels: 38 us -> 37 us
    pallas_call x1, Pallas kernels: 35.9 us -> 34.9 us  [local(): pl.pallas_call(kernel, out_shape=(jax.ShapeDtypeStruct((DZ, NR, NY), F32)...]
where the time goes in v5:
time: 37.8 us; the launch traced here: 37.6 us
  Pallas kernels  37 us (98%)
  between operations  0.64 us (2%)
    pallas_call x1, Pallas kernels, local(): pl.pallas_call(kernel, out_shape=(jax.ShapeDtypeStruct((DZ, NR, NY), F32)...  34.9 us
    pallas_call x1, Pallas kernels, local(): pl.pallas_call(write, out_shape=(jax.ShapeDtypeStruct((DZ, NR, NY), F32),...  2.15 us

profile of v5, /device:TPU:1, one launch (start us, length us, event | category | flops | bytes accessed | tf_op | source)
XLA Modules:
  0.0 37.6 jit_solution(13090493999117688351)
XLA Ops:
  0.6 34.9 %reaction_render.1 = (f32[8,64,1024]{2,1,0:T(8,128)S(1)}, f32[8,64,1024]{2,1,0:T(8,128)S(1)}, f32[3,2,1024]{2,1,0:T(2,128)S(1)}) custom-call(s32[4,4,16]{2,1,0:T(4,128)} %bricks_in.1, s32[32]{0:T(128)} %assign_in.1, f32[8,64,1024]{2,1,0:T(8,128)} %u.1, f32[8,64,1024]{2,1,0:T(8,128)} %v.1, f32[3,4,16]{2,1,0:T(4,128)} %bitcast.1, f32[4,16]{1,0:T(4,128)} %alpha_in.1), custom_call_target="tpu_custom_call" | custom-call | tf_op jit(solution)/shard_map/reaction_render/pallas_call | solution.py:545
  35.5 2.2 %write.1 = (f32[8,64,1024]{2,1,0:T(8,128)}, f32[8,64,1024]{2,1,0:T(8,128)}, f32[3,2,1024]{2,1,0:T(2,128)}) custom-call(f32[8,64,1024]{2,1,0:T(8,128)S(1)} %get-tuple-element.6.u, f32[8,64,1024]{2,1,0:T(8,128)S(1)} %get-tuple-element.7.v, f32[3,2,1024]{2,1,0:T(2,128)S(1)} %get-tuple-element.8.image), custom_call_target="tpu_custom_call" | custom-call | tf_op jit(solution)/shard_map/write/pallas_call | solution.py:588

commit v6 on v5

--- a/solution.py
+++ b/solution.py
@@ -120,6 +120,54 @@
         if n + 1 < len(rounds):
             tell(n + 1)
 
+    for ref, nz, nr in ((a, DZ + 4, NR + 16), (b, DZ + 2, NR + 8)):
+        for f in range(2):
+            for j in (0, LT + 1):
+
+                @pl.loop(0, nz)
+                def _(k):
+                    ref[f, j, k] = jnp.zeros((nr, 128), F32)
+
+    def send(src, dst, who):
+        n = len(copies)
+        c = pltpu.make_async_remote_copy(src_ref=src, dst_ref=dst, send_sem=hs.at[n], recv_sem=hr.at[n], device_id=who, device_id_type=MESH)
+        c.start()
+        copies.append(c)
+
+    wide = LT // CH
+    inner, depth = pl.ds(1, LT), pl.ds(2, DZ)
+    def layers(k, side):
+        js = pl.ds(jnp.minimum(tile(k * wide, 1 - core), tile(k * wide + wide - 1, 1 - core)), wide)
+        n = 2 * k + side
+        return pltpu.make_async_remote_copy(
+            src_ref=coded.at[side, js], dst_ref=zbuf.at[side, js], send_sem=hs.at[n], recv_sem=hr.at[n],
+            device_id=(t, (du, dd)[side]), device_id_type=MESH)
+
+    @pl.loop(0, CH)
+    def _(k):
+        @pl.loop(k * wide, (k + 1) * wide)
+        def _(e):
+            j = tile(e, 1 - core)
+            for f in range(2):
+                fetch(f, j).wait()
+                for side, z0 in ((0, DZ), (1, 2)):
+                    for i in range(2):
+                        coded[side, j, f, i] = enc(a[f, j + 1, z0 + i, pl.ds(ROW0, NR), :], 1.0)
+
+        @pl.when(k == 0)
+        def _():
+            pl.semaphore_wait(barrier, len(around))
+            tell(0)
+
+        for side in range(2):
+            layers(k, side).start()
+
+    copies = [layers(k, side) for k in range(CH) for side in range(2)]
+    send(a.at[:, inner, depth, pl.ds(ROW0 + NR - 2, 2), :], a.at[:, inner, depth, pl.ds(ROW0 - 2, 2), :], (tu, d))
+    send(a.at[:, inner, depth, pl.ds(ROW0, 2), :], a.at[:, inner, depth, pl.ds(ROW0 + NR, 2), :], (td, d))
+    for z0, z1, wz in ((DZ + 1, 1, du), (2, DZ + 2, dd)):
+        for r0, r1, wx in ((ROW0 + NR - 1, ROW0 - 1, tu), (ROW0, ROW0 + NR, td)):
+            send(a.at[:, inner, z0, pl.ds(r0, 1), :], a.at[:, inner, z1, pl.ds(r1, 1), :], (wx, wz))
     for c in smalls:
         c.wait()
     largest = color[0]
@@ -158,54 +206,6 @@
             seen = seen + mine
         order += found
 
-    for ref, nz, nr in ((a, DZ + 4, NR + 16), (b, DZ + 2, NR + 8)):
-        for f in range(2):
-            for j in (0, LT + 1):
-
-                @pl.loop(0, nz)
-                def _(k):
-                    ref[f, j, k] = jnp.zeros((nr, 128), F32)
-
-    def send(src, dst, who):
-        n = len(copies)
-        c = pltpu.make_async_remote_copy(src_ref=src, dst_ref=dst, send_sem=hs.at[n], recv_sem=hr.at[n], device_id=who, device_id_type=MESH)
-        c.start()
-        copies.append(c)
-
-    wide = LT // CH
-    inner, depth = pl.ds(1, LT), pl.ds(2, DZ)
-    def layers(k, side):
-        js = pl.ds(jnp.minimum(tile(k * wide, 1 - core), tile(k * wide + wide - 1, 1 - core)), wide)
-        n = 2 * k + side
-        return pltpu.make_async_remote_copy(
-            src_ref=coded.at[side, js], dst_ref=zbuf.at[side, js], send_sem=hs.at[n], recv_sem=hr.at[n],
-            device_id=(t, (du, dd)[side]), device_id_type=MESH)
-
-    @pl.loop(0, CH)
-    def _(k):
-        @pl.loop(k * wide, (k + 1) * wide)
-        def _(e):
-            j = tile(e, 1 - core)
-            for f in range(2):
-                fetch(f, j).wait()
-                for side, z0 in ((0, DZ), (1, 2)):
-                    for i in range(2):
-                        coded[side, j, f, i] = enc(a[f, j + 1, z0 + i, pl.ds(ROW0, NR), :], 1.0)
-
-        @pl.when(k == 0)
-        def _():
-            pl.semaphore_wait(barrier, len(around))
-            tell(0)
-
-        for side in range(2):
-            layers(k, side).start()
-
-    copies = [layers(k, side) for k in range(CH) for side in range(2)]
-    send(a.at[:, inner, depth, pl.ds(ROW0 + NR - 2, 2), :], a.at[:, inner, depth, pl.ds(ROW0 - 2, 2), :], (tu, d))
-    send(a.at[:, inner, depth, pl.ds(ROW0, 2), :], a.at[:, inner, depth, pl.ds(ROW0 + NR, 2), :], (td, d))
-    for z0, z1, wz in ((DZ + 1, 1, du), (2, DZ + 2, dd)):
-        for r0, r1, wx in ((ROW0 + NR - 1, ROW0 - 1, tu), (ROW0, ROW0 + NR, td)):
-            send(a.at[:, inner, z0, pl.ds(r0, 1), :], a.at[:, inner, z1, pl.ds(r1, 1), :], (wx, wz))
     rows_in, corners_in = copies[2 * CH : 2 * CH + 2], copies[2 * CH + 2 :]
 
     def steps(body, rs):
@@ -468,7 +468,7 @@
     zero = jnp.zeros((16, 128), F32)
     _, total = lax.fori_loop(0, 16, fold, (zero + 1.0, (zero, zero, zero)), unroll=4)
     for cc in range(3):
-        own[cc] = total[cc]
+        own[cc, 0:16] = total[cc]
         for h in range(2):
             pick[h, cc] = own[cc, pl.ds(h, 8, stride=2), :]
 
@@ -565,12 +565,12 @@
             pltpu.VMEM((2, LT, 2, 2, NR, 128), I16),
             pltpu.VMEM((LT, 4, 8, 128), I32),
             pltpu.VMEM((NR // 8, LT, 4, 8, 128), F32),
-            pltpu.VMEM((2, 4, 4, NR, 128), F32),
+            pltpu.VMEM((2, 4, 4, NR + 8, 128), F32),
             pltpu.VMEM((4, 4, 4, 16, 128), I16),
             pltpu.VMEM((4, 4, 4, 16, 128), I16),
             pltpu.VMEM((4, 4, 4, 16, 128), I16),
             pltpu.VMEM((16, 4, 16, 128), I16),
-            pltpu.VMEM((3, 16, 128), F32),
+            pltpu.VMEM((3, 24, 128), F32),
             pltpu.VMEM((2, 3, 8, 128), F32),
             pltpu.VMEM((8, 2, 16, 128), I16),
             pltpu.VMEM((4, 2, 2, 16, 128), I16),

time: 37.8 us -> 37.8 us (level)
  no operation moved by 1% of the time
where the time goes in v6:
time: 37.8 us; the launch traced here: 37.6 us
  Pallas kernels  37 us (98%)
  between operations  0.64 us (2%)
    pallas_call x1, Pallas kernels, local(): pl.pallas_call(kernel, out_shape=(jax.ShapeDtypeStruct((DZ, NR, NY), F32)...  34.8 us
    pallas_call x1, Pallas kernels, local(): pl.pallas_call(write, out_shape=(jax.ShapeDtypeStruct((DZ, NR, NY), F32),...  2.15 us

profile of v6, /device:TPU:1, one launch (start us, length us, event | category | flops | bytes accessed | tf_op | source)
XLA Modules:
  0.0 37.6 jit_solution(9125203473110141452)
XLA Ops:
  0.6 34.8 %reaction_render.1 = (f32[8,64,1024]{2,1,0:T(8,128)S(1)}, f32[8,64,1024]{2,1,0:T(8,128)S(1)}, f32[3,2,1024]{2,1,0:T(2,128)S(1)}) custom-call(s32[4,4,16]{2,1,0:T(4,128)} %bricks_in.1, s32[32]{0:T(128)} %assign_in.1, f32[8,64,1024]{2,1,0:T(8,128)} %u.1, f32[8,64,1024]{2,1,0:T(8,128)} %v.1, f32[3,4,16]{2,1,0:T(4,128)} %bitcast.1, f32[4,16]{1,0:T(4,128)} %alpha_in.1), custom_call_target="tpu_custom_call" | custom-call | tf_op jit(solution)/shard_map/reaction_render/pallas_call | solution.py:545
  35.5 2.2 %write.1 = (f32[8,64,1024]{2,1,0:T(8,128)}, f32[8,64,1024]{2,1,0:T(8,128)}, f32[3,2,1024]{2,1,0:T(2,128)}) custom-call(f32[8,64,1024]{2,1,0:T(8,128)S(1)} %get-tuple-element.6.u, f32[8,64,1024]{2,1,0:T(8,128)S(1)} %get-tuple-element.7.v, f32[3,2,1024]{2,1,0:T(2,128)S(1)} %get-tuple-element.8.image), custom_call_target="tpu_custom_call" | custom-call | tf_op jit(solution)/shard_map/write/pallas_call | solution.py:588

commit v7 on v6

--- a/solution.py
+++ b/solution.py
@@ -13,6 +13,7 @@
 LT = 8
 ROW0 = 8
 CU, AU = 2.0**-14, 2.0**-21
+MID = (0.6, 0.5)
 STEPS, SHIFT = 65534.0, 32767.0
 TOPS = (0.32 / CU, 0.32 / CU, 0.32 / CU, 0.16)
 TOP = 2.01 / CU
@@ -152,7 +153,7 @@
                 fetch(f, j).wait()
                 for side, z0 in ((0, DZ), (1, 2)):
                     for i in range(2):
-                        coded[side, j, f, i] = enc(a[f, j + 1, z0 + i, pl.ds(ROW0, NR), :], 1.0)
+                        coded[side, j, f, i] = (a[f, j + 1, z0 + i, pl.ds(ROW0, NR), :] - MID[f]).astype(jnp.bfloat16)
 
         @pl.when(k == 0)
         def _():
@@ -288,14 +289,14 @@
         first(j, ((3, 6, (0, 1)),), (1, 7, 1))
 
 
-    @pl.loop(0, LT, unroll=2)
+    @pl.loop(0, LT, unroll=4)
     def _(j):
         second(1, j, ((3, 4),), (1, 6, 1))
 
 
     hear(0)
 
-    @pl.loop(0, LT, unroll=2)
+    @pl.loop(0, LT, unroll=4)
     def _(j):
         middle(j, (1, 6, 1))
 
@@ -379,7 +380,7 @@
             for s in range(2):
                 for f in range(2):
                     for i in range(2):
-                        x = dec(zbuf[s, j, f, i], 1.0)
+                        x = zbuf[s, j, f, i].astype(F32) + MID[f]
                         a[f, j + 1, (DZ + 2) * s + i, pl.ds(ROW0, NR), :] = jnp.where(inz[s], x, 0.0)
 
         end = k == CH - 1
@@ -561,8 +562,8 @@
             pltpu.VMEM((2, LT + 2, DZ + 4, NR + 16, 128), F32),
             pltpu.VMEM((2, LT + 2, DZ + 2, NR + 8, 128), F32),
             pltpu.VMEM((2, LT, DZ, NR, 128), F32),
-            pltpu.VMEM((2, LT, 2, 2, NR, 128), I16),
-            pltpu.VMEM((2, LT, 2, 2, NR, 128), I16),
+            pltpu.VMEM((2, LT, 2, 2, NR, 128), jnp.bfloat16),
+            pltpu.VMEM((2, LT, 2, 2, NR, 128), jnp.bfloat16),
             pltpu.VMEM((LT, 4, 8, 128), I32),
             pltpu.VMEM((NR // 8, LT, 4, 8, 128), F32),
             pltpu.VMEM((2, 4, 4, NR + 8, 128), F32),

time: 37.8 us -> 37.2 us (0.984)
  Pallas kernels: 37 us -> 36.5 us
    pallas_call x1, Pallas kernels: 34.8 us -> 34.3 us  [local(): pl.pallas_call(kernel, out_shape=(jax.ShapeDtypeStruct((DZ, NR, NY), F32)...]
where the time goes in v7:
time: 37.2 us; the launch traced here: 37.1 us
  Pallas kernels  36.5 us (98%)
  between operations  0.64 us (2%)
    pallas_call x1, Pallas kernels, local(): pl.pallas_call(kernel, out_shape=(jax.ShapeDtypeStruct((DZ, NR, NY), F32)...  34.3 us
    pallas_call x1, Pallas kernels, local(): pl.pallas_call(write, out_shape=(jax.ShapeDtypeStruct((DZ, NR, NY), F32),...  2.15 us

profile of v7, /device:TPU:1, one launch (start us, length us, event | category | flops | bytes accessed | tf_op | source)
XLA Modules:
  0.0 37.1 jit_solution(2750649099416795545)
XLA Ops:
  0.6 34.3 %reaction_render.1 = (f32[8,64,1024]{2,1,0:T(8,128)S(1)}, f32[8,64,1024]{2,1,0:T(8,128)S(1)}, f32[3,2,1024]{2,1,0:T(2,128)S(1)}) custom-call(s32[4,4,16]{2,1,0:T(4,128)} %bricks_in.1, s32[32]{0:T(128)} %assign_in.1, f32[8,64,1024]{2,1,0:T(8,128)} %u.1, f32[8,64,1024]{2,1,0:T(8,128)} %v.1, f32[3,4,16]{2,1,0:T(4,128)} %bitcast.1, f32[4,16]{1,0:T(4,128)} %alpha_in.1), custom_call_target="tpu_custom_call" | custom-call | tf_op jit(solution)/shard_map/reaction_render/pallas_call | solution.py:546
  35.0 2.2 %write.1 = (f32[8,64,1024]{2,1,0:T(8,128)}, f32[8,64,1024]{2,1,0:T(8,128)}, f32[3,2,1024]{2,1,0:T(2,128)}) custom-call(f32[8,64,1024]{2,1,0:T(8,128)S(1)} %get-tuple-element.6.u, f32[8,64,1024]{2,1,0:T(8,128)S(1)} %get-tuple-element.7.v, f32[3,2,1024]{2,1,0:T(2,128)S(1)} %get-tuple-element.8.image), custom_call_target="tpu_custom_call" | custom-call | tf_op jit(solution)/shard_map/write/pallas_call | solution.py:589

commit v8 on v7

--- a/solution.py
+++ b/solution.py
@@ -21,7 +21,7 @@
 
 
 def enc(x, top):
-    return jnp.round(x * (STEPS / top) - SHIFT).astype(I32).astype(I16)
+    return ((x * (STEPS / top) + 0.5).astype(I32) - int(SHIFT)).astype(I16)
 
 
 def dec(x, top):

time: 37.2 us -> 37.3 us (level)
  no operation moved by 1% of the time
where the time goes in v8:
time: 37.3 us; the launch traced here: 37.2 us
  Pallas kernels  36.5 us (98%)
  between operations  0.64 us (2%)
    pallas_call x1, Pallas kernels, local(): pl.pallas_call(kernel, out_shape=(jax.ShapeDtypeStruct((DZ, NR, NY), F32)...  34.4 us
    pallas_call x1, Pallas kernels, local(): pl.pallas_call(write, out_shape=(jax.ShapeDtypeStruct((DZ, NR, NY), F32),...  2.15 us

profile of v8, /device:TPU:1, one launch (start us, length us, event | category | flops | bytes accessed | tf_op | source)
XLA Modules:
  0.0 37.2 jit_solution(8091117283141104567)
XLA Ops:
  0.6 34.4 %reaction_render.1 = (f32[8,64,1024]{2,1,0:T(8,128)S(1)}, f32[8,64,1024]{2,1,0:T(8,128)S(1)}, f32[3,2,1024]{2,1,0:T(2,128)S(1)}) custom-call(s32[4,4,16]{2,1,0:T(4,128)} %bricks_in.1, s32[32]{0:T(128)} %assign_in.1, f32[8,64,1024]{2,1,0:T(8,128)} %u.1, f32[8,64,1024]{2,1,0:T(8,128)} %v.1, f32[3,4,16]{2,1,0:T(4,128)} %bitcast.1, f32[4,16]{1,0:T(4,128)} %alpha_in.1), custom_call_target="tpu_custom_call" | custom-call | tf_op jit(solution)/shard_map/reaction_render/pallas_call | solution.py:546
  35.0 2.2 %write.1 = (f32[8,64,1024]{2,1,0:T(8,128)}, f32[8,64,1024]{2,1,0:T(8,128)}, f32[3,2,1024]{2,1,0:T(2,128)}) custom-call(f32[8,64,1024]{2,1,0:T(8,128)S(1)} %get-tuple-element.6.u, f32[8,64,1024]{2,1,0:T(8,128)S(1)} %get-tuple-element.7.v, f32[3,2,1024]{2,1,0:T(2,128)S(1)} %get-tuple-element.8.image), custom_call_target="tpu_custom_call" | custom-call | tf_op jit(solution)/shard_map/write/pallas_call | solution.py:589
